TPU v7x, 512 devices: a whole 4x8x8 slice. The times are simulated.
512 devices in a mesh: pool: 16 (over x_hi, z), comp: 32 (over y, x_lo, core).
Axes of the slice: x: 4 (x_hi: 2, x_lo: 2; x = x_hi * 2 + x_lo), y: 8, z: 8, core: 2. Of those that a mesh axis runs over, the one named last changes fastest.
Arguments:
- queries: bfloat16 [16, 1024, 8192], P('pool', None, 'comp'), may hold values from -512 to 512
- fresh_kv: bfloat16 [16, 1024, 32, 256], P('pool', None, 'comp'), may hold values from -8 to 8, as said below
- head_hidden: bfloat16 [16, 128, 8192], P('pool', None, 'comp'), may hold values from -4096 to 4096
- norm_gain: bfloat16 [8192], P('comp'), may hold values from 0.5 to 1.5
- kv_weight: bfloat16 [8192, 2048], P('comp'), may hold values from -0.0625 to 0.0625
- kv_store: bfloat16 [1024, 64, 32, 256], P('pool', None, 'comp'), may hold values from -8 to 8, as said below
- split_blocks: int32 [16], P('pool'), may hold values from 0 to 2
- tail_counts: int32 [16], replicated, may hold values from 32 to 64, as said below
- holder_list: int32 [16, 64], replicated, may hold values from 0 to 15, as said below
- slot_list: int32 [16, 64], replicated, may hold values from 0 to 63, as said below
Outputs:
- attention_out: bfloat16 [16, 1024, 8192], P('pool', None, 'comp')
Inputs may be any that keep to these rules, and one draw needn't show every extreme that they name: fresh_kv[:, :, r] is equal for all ranks r of one KV head, the head r // 4. kv_store[:, :, r] is equal for all ranks r of one KV head, as for fresh_kv. Slot b of holder h is row h * 64 + b. `tail_counts`: some session loads 64 blocks. `holder_list`: one holder holds at most 4 blocks of one session, and for every session some holder holds exactly 4 of its loaded blocks. `slot_list`: no two entries of any sessions share a holder and a slot.
All inputs are finite; a program needn't handle non-finite values.
Results may differ from a plain program's by a relative error of at most 0.0041.
Values may be sent and summed in bfloat16 or wider, within the bound.
No kernel may reach another device: no remote copies, remote signals or barrier semaphores. Data moves between devices by JAX's collectives and lax.ppermute only.
A program may use at most 64 MiB of HBM per device.

v0:
```python
from functools import reduce
import math

import jax
import jax.numpy as jnp
from jax import lax
from jax.sharding import PartitionSpec as P


def rotate_keys(key_rows, positions):
    half_dim = key_rows.shape[-1] // 2
    frequency = 500000.0 ** (-2.0 * jnp.arange(half_dim, dtype=jnp.float32) / key_rows.shape[-1])
    angles = positions.astype(jnp.float32)[:, None] * frequency[None, :]
    cosine = jnp.cos(angles)[:, None, :]
    sine_part = jnp.sin(angles)[:, None, :]
    first_half = key_rows[..., :half_dim]
    second = key_rows[..., half_dim:]
    return jnp.concatenate(
        [first_half * cosine - second * sine_part, second * cosine + first_half * sine_part],
        axis=-1,
    )


def segment_scores(query_block, key_part, live_part, head_dim):
    raw_scores = jnp.einsum(
        "nd,ld->nl", query_block, key_part, preferred_element_type=jnp.float32
    ) / math.sqrt(head_dim)
    return jnp.where(live_part, raw_scores, -jnp.inf)


def per_device(
    queries,
    fresh_kv,
    head_hidden,
    norm_gain,
    kv_weight,
    kv_store,
    split_blocks,
    tail_counts,
    holder_list,
    slot_list,
):
    pool_count = lax.axis_size("pool")
    pool_rank = lax.axis_index("pool")
    rank_count = lax.axis_size("comp")
    comp_rank = lax.axis_index("comp")
    head_dim = fresh_kv.shape[3] // 2
    rows_new = queries.shape[1]
    heads_here = queries.shape[2] // head_dim
    block_rows = kv_store.shape[1]
    cell_count = holder_list.shape[1]
    capacity = cell_count // pool_count
    kv_heads = kv_weight.shape[1] // (2 * head_dim)
    share_count = rank_count // kv_heads
    hidden = head_hidden[0].astype(jnp.float32)
    scaled = (hidden * norm_gain.astype(jnp.float32)).astype(jnp.bfloat16)
    squares = jnp.sum(hidden * hidden, axis=-1)
    own_head = comp_rank // share_count
    head_rows = hidden.shape[0]
    positions = jnp.arange(head_rows, dtype=jnp.int32)
    width_total = hidden.shape[1] * rank_count
    partial_value = jnp.dot(scaled, kv_weight, preferred_element_type=jnp.float32)
    summed, squares = lax.psum((partial_value, squares), "comp")
    inverse_rms = lax.rsqrt(squares / width_total + 1e-05)
    head_block = (
        lax.dynamic_slice_in_dim(summed, own_head * 2 * head_dim, 2 * head_dim, 1)
        * inverse_rms[:, None]
    )
    head_keys = rotate_keys(head_block[:, None, :head_dim], positions)[:, 0].astype(jnp.bfloat16)
    head_values = head_block[:, head_dim:].astype(jnp.bfloat16)
    cell_index = jnp.arange(cell_count, dtype=jnp.int32)
    loaded_ok = cell_index[None, :] < tail_counts[:, None]
    held_here = (holder_list == pool_rank) & loaded_ok
    order_rank = jnp.cumsum(held_here.astype(jnp.int32), axis=1) - 1
    picked = held_here[:, None, :] & (
        order_rank[:, None, :] == jnp.arange(capacity, dtype=jnp.int32)[None, :, None]
    )
    chosen = jnp.sum(jnp.where(picked, slot_list[:, None, :], 0), axis=2)
    outgoing = jnp.take(kv_store[:, :, 0, :], chosen.reshape(-1), axis=0).reshape(
        pool_count, capacity * block_rows, 2 * head_dim
    )
    own_holders = lax.dynamic_index_in_dim(holder_list, pool_rank, 0, keepdims=False)
    own_ok = lax.dynamic_index_in_dim(loaded_ok, pool_rank, 0, keepdims=False)
    pool_ids = jnp.arange(pool_count, dtype=jnp.int32)
    arrivals = jnp.sum(
        ((own_holders[None, :] == pool_ids[:, None]) & own_ok[None, :]).astype(jnp.int32), axis=1
    )
    received = lax.all_to_all(outgoing, "pool", split_axis=0, concat_axis=0, tiled=True)
    slot_live = (
        jnp.arange(capacity, dtype=jnp.int32)[None, :] < jnp.take(arrivals, pool_ids)[:, None]
    )
    loaded_live = jnp.broadcast_to(
        slot_live[:, :, None], (pool_count, capacity, block_rows)
    ).reshape(-1)
    loaded = received.reshape(pool_count * capacity * block_rows, 2 * head_dim)
    loaded_keys = loaded[:, :head_dim]
    loaded_values = loaded[:, head_dim:]
    fresh_rows = fresh_kv[0, :, 0, :]
    fresh_keys = fresh_rows[:, :head_dim]
    fresh_values = fresh_rows[:, head_dim:]
    head_live = positions < split_blocks[0] * block_rows
    query_span = min(512, rows_new)
    block_total = rows_new // query_span
    query_heads = jnp.transpose(
        queries[0].reshape(block_total, query_span, heads_here, head_dim), (2, 0, 1, 3)
    )
    query_heads = query_heads.reshape(heads_here * block_total, query_span, head_dim)
    fresh_index = jnp.arange(rows_new, dtype=jnp.int32)

    def attend(block_item):
        query_block, block_index = block_item
        first_row = block_index % block_total * query_span
        fresh_live = (
            fresh_index[None, :] <= first_row + jnp.arange(query_span, dtype=jnp.int32)[:, None]
        )
        scores = [
            segment_scores(query_block, key_part, live_part, head_dim)
            for key_part, live_part in (
                (head_keys, head_live[None, :]),
                (loaded_keys, loaded_live[None, :]),
                (fresh_keys, fresh_live),
            )
        ]
        row_peak = reduce(
            jnp.maximum, [jnp.max(score_part, axis=1, keepdims=True) for score_part in scores]
        )
        exp_terms = [jnp.exp(score_part - row_peak) for score_part in scores]
        denominator = reduce(
            jnp.add, [jnp.sum(term_part, axis=1, keepdims=True) for term_part in exp_terms]
        )
        mixed = reduce(
            jnp.add,
            [
                jnp.dot(
                    term_part.astype(jnp.bfloat16), value_part, preferred_element_type=jnp.float32
                )
                for term_part, value_part in zip(
                    exp_terms, (head_values, loaded_values, fresh_values)
                )
            ],
        )
        return (mixed / denominator).astype(jnp.bfloat16)

    outputs = lax.map(attend, (query_heads, jnp.arange(heads_here * block_total, dtype=jnp.int32)))
    attention = jnp.transpose(outputs.reshape(heads_here, rows_new, head_dim), (1, 0, 2)).reshape(
        rows_new, heads_here * head_dim
    )
    return attention[None]


def solution(mesh):
    return jax.shard_map(
        per_device,
        mesh=mesh,
        in_specs=(
            P("pool", None, "comp"),
            P("pool", None, "comp", None),
            P("pool", None, "comp"),
            P("comp"),
            P("comp", None),
            P("pool", None, "comp", None),
            P("pool"),
            P(),
            P(),
            P(),
        ),
        out_specs=P("pool", None, "comp"),
        check_vma=False,
    )
```

profile of v0, /device:TPU:1, one launch (start us, length us, event | category | flops | bytes accessed | tf_op | source)
XLA Modules:
  0.0 344.8 jit_solution(8846204513956030727)
XLA Ops:
  6.5 0.9 fusion.57
  7.5 0.2 reduce_window_sum.11
  7.7 0.8 select_reduce_fusion
  9.0 2.0 gather_fusion.1
  11.1 2.9 bitcast_select_fusion
  14.0 13.6 %all-to-all-start = ((bf16[16,256,256]{2,1,0:T(8,128)(2,1)}), bf16[16,256,256]{2,1,0:T(8,128)(2,1)}, u32[]{:S(2)}, u32[]{:S(2)}) async-start(bf16[16,256,256]{2,1,0:T(8,128)(2,1)} %bitcast_select_fusion), calls=%async_computation | async-start | bytes 4194304 | tf_op jit(solution)/shard_map/all_to_all | solution.py:88
  27.7 1.6 fusion.41
  29.3 0.8 fusion.55
  30.1 0.1 convert_reduce_fusion
  30.2 0.1 fusion.40
  30.4 1.2 reshape_squeeze.3
  31.5 0.9 copy.21
  33.1 0.7 gather_fusion
  33.7 55.5 %psum.15 = f32[128]{0:T(128)S(1)} all-reduce(f32[128]{0:T(128)S(1)} %fusion.40), channel_id=1, replica_groups=mesh['pool'=16,'comp'=32] {'comp'}, use_global_device_ids=true, to_apply=%region_3.4 | all-reduce | flops 128 | bytes 1024 | tf_op jit(solution)/shard_map/psum | solution.py:63
  89.4 0.8 fusion.61
  90.1 177.5 %all-reduce.2.cloned.1.call-done = f32[128,2048]{0,1:T(8,128)} async-done(((f32[128,2048]{0,1:T(8,128)}), f32[128,2048]{0,1:T(8,128)}) %all-reduce.2.cloned.1.call-update) | async-done | bytes 1048592 | tf_op jit(solution)/shard_map/psum | solution.py:63
  267.7 0.9 dynamic-slice_multiply_fusion
  268.6 0.2 fusion.50
  268.8 0.1 copy.25
  268.9 0.1 copy.26
  269.1 2.7 fusion.60
  271.7 63.5 %while.13 = (s32[]{:T(128)}, bf16[4,512,128]{2,1,0:T(8,128)(2,1)}, bf16[4,512,128]{2,1,0:T(8,128)(2,1)}, bf16[128,128]{1,0:T(8,128)(2,1)S(1)}, bf16[4096,128]{1,...) while((s32[]{:T(128)}, bf16[4,512,128]{2,1,0:T(8,128)(2,1)}, ...), condition=%wide.region_13.14_spmd.clone, body=%wide.region_6.13_spmd.clone.sunk | while | flops 1403715200 | bytes 49160856 | solution.py:144
  271.8 0.7 dynamic_slice.60
  274.5 2.9 fusion.96
  277.6 2.3 fusion.98
  279.9 1.1 fusion.97
  281.1 2.2 fusion.103
  283.2 0.5 fusion.101
  283.8 0.6 copy-done.3
  284.4 1.8 fusion.100
  286.2 0.5 fusion.99
  286.7 0.9 fusion.104
  287.6 0.7 dynamic_slice.60
  290.4 2.9 fusion.96
  293.4 2.3 fusion.98
  295.8 1.1 fusion.97
  296.9 2.2 fusion.103
  299.1 0.5 fusion.101
  299.7 0.6 copy-done.3
  300.3 1.8 fusion.100
  302.1 0.5 fusion.99
  302.6 0.9 fusion.104
  303.5 0.7 dynamic_slice.60
  306.2 2.9 fusion.96
  309.3 2.3 fusion.98
  311.6 1.1 fusion.97
  312.8 2.2 fusion.103
  315.0 0.5 fusion.101
  315.5 0.6 copy-done.3
  316.2 1.8 fusion.100
  317.9 0.5 fusion.99
  318.4 0.9 fusion.104
  319.3 0.7 dynamic_slice.60
  322.1 2.9 fusion.96
  325.2 2.3 fusion.98
  327.5 1.1 fusion.97
  328.6 2.2 fusion.103
  330.8 0.5 fusion.101
  331.4 0.6 copy-done.3
  332.0 1.8 fusion.100
  333.8 0.5 fusion.99
  334.3 0.9 fusion.104
  335.2 1.6 copy.30
  336.8 1.1 broadcast_in_dim_reshape.4
  (76 shorter events, 1.7 us)
Async XLA Ops:
  6.5 2.5 copy-start
  14.0 13.7 %copy-start.6 = (bf16[256]{0:T(256)(128)(2,1)S(1)}, bf16[256]{0:T(256)(128)(2,1)}, u32[]{:S(2)}) copy-start(bf16[256]{0:T(256)(128)(2,1)} %param.15) | copy-start | bytes 1540
  14.0 13.7 %copy-start.2 = (bf16[256,2048]{1,0:T(8,128)(2,1)S(1)}, bf16[256,2048]{1,0:T(8,128)(2,1)}, u32[]{:S(2)}) copy-start(bf16[256,2048]{1,0:T(8,128)(2,1)} %param.16) | copy-start | bytes 3145732
  14.0 13.7 %copy-start.5 = (bf16[1,128,256]{2,1,0:T(8,128)(2,1)S(1)}, bf16[1,128,256]{2,1,0:T(8,128)(2,1)}, u32[]{:S(2)}) copy-start(bf16[1,128,256]{2,1,0:T(8,128)(2,1)} %param.14) | copy-start | bytes 196612
  14.0 255.1 %all-to-all-start = ((bf16[16,256,256]{2,1,0:T(8,128)(2,1)}), bf16[16,256,256]{2,1,0:T(8,128)(2,1)}, u32[]{:S(2)}, u32[]{:S(2)}) async-start(bf16[16,256,256]{2,1,0:T(8,128)(2,1)} %bitcast_select_fusion), calls=%async_computation | async-start | bytes 4194304 | tf_op jit(solution)/shard_map/all_to_all | solution.py:88
  27.6 240.0 %all-reduce.2.cloned.1.call-start = ((), (), s32[]{:S(2)}) async-start(), calls=%async_computation.1 | async-start | bytes 2097152 | tf_op jit(solution)/shard_map/psum | solution.py:63
  29.3 60.1 %copy-start.4 = (bf16[1,1024,1,256]{3,1,2,0:T(8,128)(2,1)S(1)}, bf16[1,1024,1,256]{3,1,2,0:T(8,128)(2,1)}, u32[]{:S(2)}) copy-start(bf16[1,1024,1,256]{3,1,2,0:T(8,128)(2,1)} %param.13) | copy-start | bytes 1572868
  281.0 2.2 copy-start.1
  283.2 1.2 copy-start.3
  296.9 2.2 copy-start.1
  299.1 1.2 copy-start.3
  312.8 2.2 copy-start.1
  314.9 1.2 copy-start.3
  328.6 2.2 copy-start.1
  330.8 1.2 copy-start.3
Sparse Core Ops, SparseCore 0:
  31.4 236.2 all-reduce.1
where the time goes:
time: 346 us; the launch traced here: 345 us
  waiting for transfers between devices  178 us (51%)
  blocking collectives  55.5 us (16%)
  matrix products  39.5 us (11%)
  local copies, waits for them, and re-layouts  18.2 us (5%)
  other arithmetic  17.4 us (5%)
  between operations  14.3 us (4%)
  starting transfers between devices  13.7 us (4%)
  loops' own time  8.63 us (2%)
    psum x1, waiting for transfers between devices, per_device(): summed, squares = lax.psum((partial_value, squares), 'comp')  178 us
    psum x1, blocking collectives, per_device(): summed, squares = lax.psum((partial_value, squares), 'comp')  55.5 us
    dot_general x12, matrix products, segment_scores(): jnp.einsum('nd,ld->nl', query_block, key_part, preferred_element_type=jnp...  25.3 us
    all_to_all x1, starting transfers between devices, per_device(): lax.all_to_all(outgoing, 'pool', split_axis=0, concat_axis=0, tiled=True)  13.6 us
    dot_general x12, matrix products, attend(): jnp.dot(term_part.astype(jnp.bfloat16), value_part, preferred_element_typ...  12.6 us
    reduce_sum x12, other arithmetic, attend(): jnp.sum(term_part, axis=1, keepdims=True)  10.9 us
    another operation x1, loops' own time, per_device(): lax.map(attend, (query_heads, jnp.arange(heads_here * block_total, dtype=...  8.63 us
  transfers between devices with their start and end apart: 2, of which 1 were waited for; matrix products, arithmetic and copies ran while one was open for 2% of the time, Pallas kernels for 0%

commit v1 on v0

v1 whole, which is shorter than its diff:
```python
import functools
import math

import jax
import jax.numpy as jnp
from jax import lax
from jax.experimental import pallas as pl
from jax.experimental.pallas import tpu as pltpu
from jax.sharding import Mesh, PartitionSpec as P

F32 = jnp.float32
BF16 = jnp.bfloat16
NT = (((1,), (1,)), ((), ()))
LOW = -1e30
VMEM_LIMIT = 56 * 2**20
QUAD = ("xl", "core")
COMP = ("y", "xl", "core")
POOL = ("xh", "z")


def params():
    return pltpu.CompilerParams(vmem_limit_bytes=VMEM_LIMIT)


def pack_kernel(me_ref, tail_ref, holder_ref, slot_ref, store_ref, out_ref, index_vmem, index_smem, sem, sems):
    sessions, cells = holder_ref.shape
    share = out_ref.shape[1] // store_ref.shape[1]
    rows = store_ref.shape[1]
    row = lax.broadcasted_iota(jnp.int32, (sessions, cells), 0)
    cell = lax.broadcasted_iota(jnp.int32, (sessions, cells), 1)
    tails = jnp.zeros((sessions, cells), jnp.int32)
    for s in range(sessions):
        tails = jnp.where(row == s, tail_ref[s], tails)
    held = (holder_ref[...] == me_ref[0]) & (cell < tails)
    before = lax.broadcasted_iota(jnp.int32, (cells, cells), 0)
    until = lax.broadcasted_iota(jnp.int32, (cells, cells), 1)
    order = jnp.dot(
        jnp.where(held, 1.0, 0.0).astype(BF16),
        jnp.where(before <= until, 1.0, 0.0).astype(BF16),
        preferred_element_type=F32,
    )
    lane = lax.broadcasted_iota(jnp.int32, (sessions, 128), 1)
    packed = jnp.zeros((sessions, 128), jnp.int32)
    for k in range(share):
        wanted = (me_ref[1] * share + k + 1).astype(F32)
        pick = jnp.where(held & (order == wanted), slot_ref[...], 0)
        packed = jnp.where(lane == k, jnp.sum(pick, axis=1, keepdims=True), packed)
    index_vmem[...] = packed
    copy = pltpu.make_async_copy(index_vmem, index_smem, sem)
    copy.start()
    copy.wait()

    def block_copy(s, k):
        return pltpu.make_async_copy(
            store_ref.at[index_smem[s, k]], out_ref.at[s, pl.ds(k * rows, rows)], sems.at[s * share + k]
        )

    for s in range(sessions):
        for k in range(share):
            block_copy(s, k).start()
    for s in range(sessions):
        for k in range(share):
            block_copy(s, k).wait()


def pack_blocks(me, tail_counts, holder_list, slot_list, store, share):
    sessions, cells = holder_list.shape
    _, rows, width = store.shape
    whole = pl.BlockSpec(memory_space=pltpu.VMEM)
    return pl.pallas_call(
        pack_kernel,
        out_shape=jax.ShapeDtypeStruct((sessions, share * rows, width), store.dtype),
        in_specs=[
            pl.BlockSpec(memory_space=pltpu.SMEM),
            pl.BlockSpec(memory_space=pltpu.SMEM),
            whole,
            whole,
            pl.BlockSpec(memory_space=pl.ANY),
        ],
        out_specs=pl.BlockSpec(memory_space=pl.ANY),
        scratch_shapes=[
            pltpu.VMEM((sessions, 128), jnp.int32),
            pltpu.SMEM((sessions, 128), jnp.int32),
            pltpu.SemaphoreType.DMA(()),
            pltpu.SemaphoreType.DMA((sessions * share,)),
        ],
        compiler_params=params(),
        name="pack_blocks",
    )(me, tail_counts, holder_list, slot_list, store)


def project_kernel(hidden_ref, gain_ref, weight_ref, out_ref):
    hidden = hidden_ref[...].astype(F32)
    rows = hidden.shape[0]
    quarter = out_ref.shape[1] - 16
    parts = rows // quarter
    width = out_ref.shape[2]
    scaled = (hidden * gain_ref[...].astype(F32)).astype(BF16)
    squares = lax.dot_general(
        jnp.ones((16, hidden.shape[1]), F32), hidden * hidden, NT,
        precision=lax.Precision.HIGHEST, preferred_element_type=F32,
    )
    high = squares.astype(BF16)
    low = (squares - high.astype(F32)).astype(BF16)
    tail = jnp.concatenate([high, low], axis=1)
    for head in range(weight_ref.shape[1] // width):
        part = jnp.dot(
            scaled, weight_ref[:, head * width : (head + 1) * width], preferred_element_type=F32
        ).astype(BF16)
        for t in range(parts):
            out_ref[head * parts + t, :quarter, :] = part[t * quarter : (t + 1) * quarter]
            out_ref[head * parts + t, quarter:, :] = tail


def project(hidden, gain, weight, heads, parts):
    rows = hidden.shape[0]
    width = weight.shape[1] // heads
    return pl.pallas_call(
        project_kernel,
        out_shape=jax.ShapeDtypeStruct((heads * parts, rows // parts + 16, width), BF16),
        compiler_params=params(),
        name="project",
    )(hidden, gain, weight)


def finish_kernel(width_total, quad_ref, recv_ref, cos_ref, sin_ref, out_ref):
    rows, width = out_ref.shape
    half = width // 2
    total = recv_ref[0].astype(F32)
    for i in range(1, recv_ref.shape[0]):
        total = total + recv_ref[i].astype(F32)
    lane = lax.broadcasted_iota(jnp.int32, (rows, half), 1)
    row = lax.broadcasted_iota(jnp.int32, (rows, half), 0)
    squares = total[rows : rows + 1, :half] + total[rows : rows + 1, half:]
    squares = jnp.sum(
        jnp.where(lane == row + quad_ref[0] * rows, squares, 0.0), axis=1, keepdims=True
    )
    block = total[:rows] * lax.rsqrt(squares / width_total + 1e-05)
    keys = block[:, :half]
    swapped = jnp.concatenate([keys[:, half // 2 :], keys[:, : half // 2]], axis=1)
    out_ref[:, :half] = (keys * cos_ref[...] + swapped * sin_ref[...]).astype(BF16)
    out_ref[:, half:] = block[:, half:].astype(BF16)


def finish(width_total, quad, received, cosine, sine):
    vmem = pl.BlockSpec(memory_space=pltpu.VMEM)
    return pl.pallas_call(
        functools.partial(finish_kernel, width_total),
        out_shape=jax.ShapeDtypeStruct((received.shape[1] - 16, received.shape[2]), BF16),
        in_specs=[pl.BlockSpec(memory_space=pltpu.SMEM), vmem, vmem, vmem],
        out_specs=vmem,
        compiler_params=params(),
        name="finish_head",
    )(quad, received, cosine, sine)


def scaled_queries(queries, head_dim):
    scaled = queries.astype(F32) * (math.log2(math.e) / math.sqrt(head_dim))
    high = scaled.astype(BF16)
    low = (scaled - high.astype(F32)).astype(BF16)
    return jnp.concatenate([high, low], axis=1)


def fresh_kernel(block, queries_ref, fresh_ref, mixed_ref, stats_ref):
    rows, width = queries_ref.shape
    head_dim = fresh_ref.shape[1] // 2
    heads = width // head_dim
    lane = lax.broadcasted_iota(jnp.int32, (block, 128), 1)
    row = lax.broadcasted_iota(jnp.int32, (block, block), 0)
    column = lax.broadcasted_iota(jnp.int32, (block, block), 1)
    for b in range(rows // block):
        here = pl.ds(b * block, block)
        reach = (b + 1) * block
        keys = fresh_ref[:reach, :head_dim]
        keys = jnp.concatenate([keys, keys], axis=1)
        values = fresh_ref[:reach, head_dim:]
        values = jnp.concatenate([values, jnp.ones_like(values)], axis=1)
        stats = jnp.zeros((block, 128), F32)
        for h in range(heads):
            query = scaled_queries(queries_ref[here, h * head_dim : (h + 1) * head_dim], head_dim)
            scores = lax.dot_general(query, keys, NT, preferred_element_type=F32)
            last = jnp.where(column <= row, scores[:, b * block :], LOW)
            if b:
                scores = jnp.concatenate([scores[:, : b * block], last], axis=1)
            else:
                scores = last
            peak = jnp.max(scores, axis=1, keepdims=True)
            terms = jnp.exp2(scores - peak).astype(BF16)
            mixed = jnp.dot(terms, values, preferred_element_type=F32)
            mixed_ref[here, h * head_dim : (h + 1) * head_dim] = mixed[:, :head_dim]
            stats = jnp.where(lane == 2 * h, peak, stats)
            stats = jnp.where(lane == 2 * h + 1, mixed[:, head_dim:], stats)
        stats_ref[here, :] = stats


def attend_fresh(queries, fresh):
    rows, width = queries.shape
    return pl.pallas_call(
        functools.partial(fresh_kernel, min(256, rows)),
        out_shape=(
            jax.ShapeDtypeStruct((rows, width), F32),
            jax.ShapeDtypeStruct((rows, 128), F32),
        ),
        compiler_params=params(),
        cost_estimate=pl.CostEstimate(flops=2 * 2**30, bytes_accessed=2**21, transcendentals=2**20),
        name="attend_fresh",
    )(queries, fresh)


def loaded_kernel(
    chunk, counts_ref, queries_ref, own_ref, other_ref, head_ref, mixed_ref, stats_ref, out_ref, keys_all, values_all
):
    holders, slab, width = own_ref.shape
    head_dim = width // 2
    head_rows = head_ref.shape[0]
    loaded_rows = 2 * holders * slab
    share = 2
    rows = slab // share
    full = counts_ref[holders]
    live_rows = counts_ref[holders + 1]
    core = counts_ref[holders + 2]

    @pl.when(pl.program_id(0) == 0)
    def _():
        def fill(holder, _):
            count = counts_ref[holder]
            for side, ref in enumerate((own_ref, other_ref)):
                for k in range(share):
                    place = jnp.where(core == side, k, share + k)
                    live = place < count
                    source = jnp.where(live, holder, full)
                    block = ref[source, k * rows : (k + 1) * rows, :]
                    weight = jnp.where(live, 1.0, 0.0).astype(BF16)
                    start = pl.multiple_of(side * holders * slab + holder * slab + k * rows, rows)
                    here = pl.ds(start, rows)
                    keys_all[here, :head_dim] = block[:, :head_dim]
                    keys_all[here, head_dim:] = block[:, :head_dim]
                    values_all[here, :head_dim] = block[:, head_dim:] * weight
                    values_all[here, head_dim:] = jnp.full((rows, head_dim), weight, BF16)
            return 0

        lax.fori_loop(0, holders, fill, 0)
        position = lax.broadcasted_iota(jnp.int32, (head_rows, head_dim), 0)
        admitted = position < live_rows
        spare = jnp.broadcast_to(own_ref[full, 0:1, :head_dim].astype(F32), (head_rows, head_dim))
        keys = jnp.where(admitted, head_ref[:, :head_dim].astype(F32), spare).astype(BF16)
        keys_all[loaded_rows:, :head_dim] = keys
        keys_all[loaded_rows:, head_dim:] = keys
        values = jnp.where(admitted, head_ref[:, head_dim:].astype(F32), 0.0).astype(BF16)
        values_all[loaded_rows:, :head_dim] = values
        values_all[loaded_rows:, head_dim:] = jnp.where(admitted, 1.0, 0.0).astype(BF16)

    heads = queries_ref.shape[1] // head_dim
    query = [
        scaled_queries(queries_ref[:, h * head_dim : (h + 1) * head_dim], head_dim) for h in range(heads)
    ]
    peak = [stats_ref[:, 2 * h : 2 * h + 1] for h in range(heads)]
    mixed = [
        jnp.concatenate(
            [
                mixed_ref[:, h * head_dim : (h + 1) * head_dim],
                jnp.broadcast_to(stats_ref[:, 2 * h + 1 : 2 * h + 2], (queries_ref.shape[0], head_dim)),
            ],
            axis=1,
        )
        for h in range(heads)
    ]
    starts = list(range(0, loaded_rows, chunk))
    for start in starts:
        stop = start + chunk if start != starts[-1] else loaded_rows + head_rows
        for h in range(heads):
            scores = lax.dot_general(query[h], keys_all[start:stop, :], NT, preferred_element_type=F32)
            higher = jnp.maximum(peak[h], jnp.max(scores, axis=1, keepdims=True))
            terms = jnp.exp2(scores - higher).astype(BF16)
            mixed[h] = mixed[h] * jnp.exp2(peak[h] - higher) + jnp.dot(
                terms, values_all[start:stop, :], preferred_element_type=F32
            )
            peak[h] = higher
    for h in range(heads):
        out_ref[:, h * head_dim : (h + 1) * head_dim] = (
            mixed[h][:, :head_dim] / mixed[h][:, head_dim:]
        ).astype(BF16)


def attend_loaded(counts, queries, own, other, head, mixed, stats):
    rows, width = queries.shape
    block = min(512, rows)
    total = own.shape[0] * own.shape[1] * 2 + head.shape[0]
    whole = lambda shape: pl.BlockSpec(shape, lambda i, counts: (0,) * len(shape))
    rowed = lambda columns: pl.BlockSpec((block, columns), lambda i, counts: (i, 0))
    return pl.pallas_call(
        functools.partial(loaded_kernel, 512),
        grid_spec=pltpu.PrefetchScalarGridSpec(
            num_scalar_prefetch=1,
            grid=(rows // block,),
            in_specs=[
                rowed(width),
                whole(own.shape),
                whole(other.shape),
                whole(head.shape),
                rowed(width),
                rowed(128),
            ],
            out_specs=rowed(width),
            scratch_shapes=[pltpu.VMEM((total, 256), BF16), pltpu.VMEM((total, 256), BF16)],
        ),
        out_shape=jax.ShapeDtypeStruct((rows, width), BF16),
        compiler_params=params(),
        name="attend_loaded",
    )(counts, queries, own, other, head, mixed, stats)


def per_device(
    queries,
    fresh_kv,
    head_hidden,
    norm_gain,
    kv_weight,
    kv_store,
    split_blocks,
    tail_counts,
    holder_list,
    slot_list,
):
    pool_rank = lax.axis_index(POOL)
    core = lax.axis_index("core")
    quad = lax.axis_index(QUAD)
    quads = lax.axis_size(QUAD)
    holders = lax.axis_size(POOL)
    heads = lax.axis_size("y")
    ranks = lax.axis_size(COMP)
    cells = holder_list.shape[1]
    capacity = cells // holders
    block_rows = kv_store.shape[1]
    head_dim = kv_store.shape[3] // 2
    head_rows = head_hidden.shape[1]

    store = kv_store[:, :, 0, :]
    me = jnp.stack([pool_rank, core]).astype(jnp.int32)
    outgoing = pack_blocks(me, tail_counts, holder_list, slot_list, store, capacity // 2)
    own = lax.all_to_all(outgoing, POOL, split_axis=0, concat_axis=0, tiled=True)

    partial_sums = project(head_hidden[0], norm_gain[None, :], kv_weight, heads, quads)
    partial_sums = lax.all_to_all(partial_sums, COMP, split_axis=0, concat_axis=0, tiled=True)

    mixed, stats = attend_fresh(queries[0], fresh_kv[0, :, 0, :])

    quarter = head_rows // quads
    positions = (quad * quarter + jnp.arange(quarter, dtype=jnp.int32)).astype(F32)
    frequency = 500000.0 ** (-2.0 * jnp.arange(head_dim // 2, dtype=F32) / head_dim)
    angles = positions[:, None] * frequency[None, :]
    cosine = jnp.cos(angles)
    sine = jnp.sin(angles)
    cosine = jnp.concatenate([cosine, cosine], axis=1)
    sine = jnp.concatenate([-sine, sine], axis=1)
    head = finish(
        head_hidden.shape[2] * ranks, quad.astype(jnp.int32)[None], partial_sums, cosine, sine
    )
    head = lax.all_gather(head, QUAD, axis=0, tiled=True)

    own_holders = lax.dynamic_index_in_dim(holder_list, pool_rank, 0, keepdims=False)
    own_ok = jnp.arange(cells, dtype=jnp.int32) < lax.dynamic_index_in_dim(
        tail_counts, pool_rank, 0, keepdims=False
    )
    holder_ids = jnp.arange(holders, dtype=jnp.int32)
    counts = jnp.sum(
        ((own_holders[None, :] == holder_ids[:, None]) & own_ok[None, :]).astype(jnp.int32), axis=1
    )
    counts = jnp.concatenate(
        [
            counts,
            jnp.argmax(counts).astype(jnp.int32)[None],
            split_blocks * block_rows,
            core.astype(jnp.int32)[None],
        ]
    )
    other = lax.ppermute(own, "core", [(0, 1), (1, 0)])
    return attend_loaded(counts, queries[0], own, other, head, mixed, stats)[None]


def solution(mesh):
    fine = Mesh(mesh.devices.reshape(2, 8, 8, 2, 2), ("xh", "z", "y", "xl", "core"))
    return jax.shard_map(
        per_device,
        mesh=fine,
        in_specs=(
            P(POOL, None, COMP),
            P(POOL, None, COMP, None),
            P(POOL, None, COMP),
            P(COMP),
            P(COMP, None),
            P(POOL, None, COMP, None),
            P(POOL),
            P(),
            P(),
            P(),
        ),
        out_specs=P(POOL, None, COMP),
        check_vma=False,
    )
```

time: 346 us -> 142 us (0.41)
  waiting for transfers between devices: 178 us -> 33.9 us
  Pallas kernels: 0 us -> 65.7 us
  blocking collectives: 55.5 us -> 7.91 us
  matrix products: 39.5 us -> 0 us
  local copies, waits for them, and re-layouts: 18.2 us -> 3.75 us
  between operations: 14.3 us -> 0.74 us
  other arithmetic: 17.4 us -> 4.21 us
  starting transfers between devices: 13.7 us -> 25.5 us
  loops' own time: 8.63 us -> 0 us
    psum x1 -> x0, waiting for transfers between devices: 178 us -> none  [per_device(): summed, squares = lax.psum((partial_value, squares), 'comp')]
    pallas_call x0 -> x5, Pallas kernels: none -> 65.7 us  [the longest x1 34.9 us: pack_blocks(): pl.pallas_call(pack_kernel, out_shape=jax.ShapeDtypeStruct((sessions, sha...]
    psum x1 -> x0, blocking collectives: 55.5 us -> none  [per_device(): summed, squares = lax.psum((partial_value, squares), 'comp')]
    dot_general x25 -> x0, matrix products: 39.5 us -> none  [the longest x12 25.3 us: segment_scores(): jnp.einsum('nd,ld->nl', query_block, key_part, preferred_element_type=jnp...]
    all_to_all x1 -> x2, waiting for transfers between devices: 0.01 us -> 33.9 us  [the longest x1 23.8 us: per_device(): lax.all_to_all(outgoing, POOL, split_axis=0, concat_axis=0, tiled=True)]
    reduce_sum x15 -> x1, other arithmetic: 12 us -> 0.12 us  [per_device(): jnp.sum(((own_holders[None, :] == holder_ids[:, None]) & own_ok[None, :])...]
    all_to_all x1 -> x2, starting transfers between devices: 13.6 us -> 23.3 us  [the longest x1 13.4 us: per_device(): lax.all_to_all(outgoing, POOL, split_axis=0, concat_axis=0, tiled=True)]
    another operation x1 -> x0, loops' own time: 8.63 us -> none  [per_device(): lax.map(attend, (query_heads, jnp.arange(heads_here * block_total, dtype=...]
  transfers between devices with their start and end apart: 2 -> 3, of which waited for: 1 -> 2; matrix products, arithmetic and copies ran while one was open for 2% -> 4% of each run, Pallas kernels for 0% -> 7%
where the time goes in v1:
time: 142 us
  Pallas kernels  65.7 us (46%)
  waiting for transfers between devices  33.9 us (24%)
  starting transfers between devices  25.5 us (18%)
  blocking collectives  7.91 us (6%)
  other arithmetic  4.21 us (3%)
  local copies, waits for them, and re-layouts  3.75 us (3%)
    pallas_call x1, Pallas kernels, pack_blocks(): pl.pallas_call(pack_kernel, out_shape=jax.ShapeDtypeStruct((sessions, sha...  34.9 us
    all_to_all x1, waiting for transfers between devices, per_device(): lax.all_to_all(outgoing, POOL, split_axis=0, concat_axis=0, tiled=True)  23.8 us
    pallas_call x1, Pallas kernels, attend_loaded(): pl.pallas_call(functools.partial(loaded_kernel, 512), grid_spec=pltpu.Pre...  21.6 us
    all_to_all x1, starting transfers between devices, per_device(): lax.all_to_all(outgoing, POOL, split_axis=0, concat_axis=0, tiled=True)  13.4 us
    all_to_all x1, waiting for transfers between devices, per_device(): lax.all_to_all(partial_sums, COMP, split_axis=0, concat_axis=0, tiled=True)  10.1 us
    all_to_all x1, starting transfers between devices, per_device(): lax.all_to_all(partial_sums, COMP, split_axis=0, concat_axis=0, tiled=True)  9.88 us
    all_gather x1, blocking collectives, per_device(): head = lax.all_gather(head, QUAD, axis=0, tiled=True)  7.91 us
    pallas_call x1, Pallas kernels, attend_fresh(): pl.pallas_call(functools.partial(fresh_kernel, min(256, rows)), out_shape...  4.75 us
  transfers between devices with their start and end apart: 3, of which 2 were waited for; matrix products, arithmetic and copies ran while one was open for 4% of the time, Pallas kernels for 7%

profile of v1, /device:TPU:1, one launch (start us, length us, event | category | flops | bytes accessed | tf_op | source)
XLA Modules:
  0.0 141.7 jit_solution(5848243672628676260)
XLA Ops:
  0.0 0.6 pad_add_fusion.1.me_ref
  0.6 0.0 copy-start.4
  0.6 34.9 %pack_blocks.1 = bf16[16,128,256]{2,1,0:T(8,128)(2,1)} custom-call(s32[2]{0:T(128)} %pad_add_fusion.1.me_ref, s32[16]{0:T(128)} %tail_ref.1, s32[16,64]{1,0:T(8,128)} %holder_ref.1, s32[16,64]{1,0:T(8,128)} %slot_ref.1, bf16[64,64,256]{2,1,0:T(8,128)(2,1)} %bitcast.12), custom_call_target="tpu_custom_call" | custom-call | tf_op jit(solution)/shard_map/pack_blocks/pallas_call | solution.py:70
  35.4 13.4 %all-to-all-start = ((bf16[16,128,256]{2,1,0:T(8,128)(2,1)}), bf16[16,128,256]{2,1,0:T(8,128)(2,1)S(1)}, u32[]{:S(2)}, u32[]{:S(2)}) async-start(bf16[16,128,256]{2,1,0:T(8,128)(2,1)} %pack_blocks.1), calls=%async_computation | async-start | bytes 2097152 | tf_op jit(solution)/shard_map/all_to_all | solution.py:341
  48.9 0.0 copy-done.4
  48.9 0.0 copy-start.3
  48.9 0.6 broadcast_in_dim.23.gain_ref
  49.5 2.6 %project.1 = bf16[32,48,256]{2,1,0:T(8,128)(2,1)} custom-call(bf16[128,256]{1,0:T(8,128)(2,1)} %bitcast.15, bf16[1,256]{1,0:T(2,128)(2,1)} %broadcast_in_dim.23.gain_ref, bf16[256,2048]{1,0:T(8,128)(2,1)} %weight_ref.1), custom_call_target="tpu_custom_call" | custom-call | tf_op jit(solution)/shard_map/project/pallas_call | solution.py:118
  52.1 23.8 %all-to-all-done.own_ref = bf16[16,128,256]{2,1,0:T(8,128)(2,1)S(1)} async-done(((bf16[16,128,256]{2,1,0:T(8,128)(2,1)}), bf16[16,128,256]{2,1,0:T(8,128)(2,1)S(1)}, u32[]{:S(2)}, u32[]{:S(2)}) %all-to-all-start) | async-done | bytes 1048608 | tf_op jit(solution)/shard_map/all_to_all | solution.py:341
  75.8 0.0 copy-start
  75.8 9.9 %all-to-all-start.1 = ((bf16[32,48,256]{2,1,0:T(8,128)(2,1)}), bf16[32,48,256]{2,1,0:T(8,128)(2,1)S(1)}, u32[]{:S(2)}, u32[]{:S(2)}) async-start(bf16[32,48,256]{2,1,0:T(8,128)(2,1)} %project.1), calls=%async_computation.1 | async-start | bytes 1572864 | tf_op jit(solution)/shard_map/all_to_all | solution.py:344
  85.7 0.0 copy-done.3
  85.7 0.6 dynamic_slice.9
  86.3 0.7 dynamic-slice_bitcast_fusion
  87.0 0.7 iota_compare_fusion.1
  87.7 2.1 %collective-permute-start = (bf16[16,128,256]{2,1,0:T(8,128)(2,1)S(1)}, bf16[16,128,256]{2,1,0:T(8,128)(2,1)S(1)}, u32[]{:S(2)}, u32[]{:S(2)}) collective-permute-start(bf16[16,128,256]{2,1,0:T(8,128)(2,1)S(1)} %all-to-all-done.own_ref), channel_id=1, source_target_pairs={{0,1},{1,0},{2,3},{3,2},{4,5},{5,4},{6,7},{7,6},{8,9},{9,8},{10,11... | collective-permute-start | bytes 3145736 | tf_op jit(solution)/shard_map/ppermute | solution.py:377
  90.5 0.1 convert_reduce_fusion
  90.6 0.7 iota_reduce_fusion
  91.3 1.3 pad_add_fusion.counts_ref
  92.6 0.1 fusion.1
  92.8 0.7 pad_maximum_fusion
  93.5 4.7 %attend_fresh.1 = (f32[1024,256]{1,0:T(8,128)}, f32[1024,128]{1,0:T(8,128)}) custom-call(bf16[1024,256]{1,0:T(8,128)(2,1)} %bitcast.13, bf16[1024,256]{1,0:T(8,128)(2,1)} %bitcast.16), custom_call_target="tpu_custom_call" | custom-call | flops 2147483648 | bytes 2097152 | tf_op jit(solution)/shard_map/attend_fresh/pallas_call | solution.py:198
  98.2 0.0 copy-done
  98.2 10.1 %all-to-all-done.1.recv_ref = bf16[32,48,256]{2,1,0:T(8,128)(2,1)S(1)} async-done(((bf16[32,48,256]{2,1,0:T(8,128)(2,1)}), bf16[32,48,256]{2,1,0:T(8,128)(2,1)S(1)}, u32[]{:S(2)}, u32[]{:S(2)}) %all-to-all-start.1) | async-done | bytes 786464 | tf_op jit(solution)/shard_map/all_to_all | solution.py:344
  108.3 0.0 copy-start.1
  108.3 0.9 copy-done.1
  109.2 1.9 %finish_head.1 = bf16[32,256]{1,0:T(8,128)(2,1)} custom-call(s32[1]{0:T(128)} %bitcast.7.quad_ref, bf16[32,48,256]{2,1,0:T(8,128)(2,1)} %copy-done.1, f32[32,128]{1,0:T(8,128)} %get-tuple-element.14.cos_ref, f32[32,128]{1,0:T(8,128)} %get-tuple-element.15.sin_ref), custom_call_target="tpu_custom_call" | custom-call | tf_op jit(solution)/shard_map/finish_head/pallas_call | solution.py:147
  111.2 7.9 %all_gather.3.head_ref = bf16[128,256]{1,0:T(8,128)(2,1)} all-gather(bf16[32,256]{1,0:T(8,128)(2,1)} %finish_head.1), channel_id=1, replica_groups=mesh['xh'=2,'z'=8,'y'=8,'xl'=2,'core'=2] {'xl','core'}, dimensions={0}, use_global_device_ids=true | all-gather | bytes 81920 | tf_op jit(solution)/shard_map/all_gather | solution.py:359
  119.1 0.0 collective-permute-done.other_ref
  119.1 0.0 copy-start.2
  119.1 1.0 copy-done.2
  120.1 21.6 %attend_loaded.1 = bf16[1024,256]{1,0:T(8,128)(2,1)} custom-call(s32[19]{0:T(128)} %pad_add_fusion.counts_ref, bf16[1024,256]{1,0:T(8,128)(2,1)} %bitcast.14, bf16[16,128,256]{2,1,0:T(8,128)(2,1)} %copy-done, bf16[16,128,256]{2,1,0:T(8,128)(2,1)} %copy-done.2, bf16[128,256]{1,0:T(8,128)(2,1)} %all_gather.3.head_ref, f32[1024,256]{1,0:T(8,128)} %get-tuple-element.9.mixed_ref, ...), custom_call_target="tpu_custom_call" | custom-call | tf_op jit(solution)/shard_map/attend_loaded/pallas_call | solution.py:291
  (2 shorter events, 0.0 us)
Async XLA Ops:
  0.6 48.3 %copy-start.4 = (bf16[256]{0:T(256)(128)(2,1)S(1)}, bf16[256]{0:T(256)(128)(2,1)}, u32[]{:S(2)}) copy-start(bf16[256]{0:T(256)(128)(2,1)} %param.13) | copy-start | bytes 1540
  35.4 40.4 %all-to-all-start = ((bf16[16,128,256]{2,1,0:T(8,128)(2,1)}), bf16[16,128,256]{2,1,0:T(8,128)(2,1)S(1)}, u32[]{:S(2)}, u32[]{:S(2)}) async-start(bf16[16,128,256]{2,1,0:T(8,128)(2,1)} %pack_blocks.1), calls=%async_computation | async-start | bytes 2097152 | tf_op jit(solution)/shard_map/all_to_all | solution.py:341
  48.9 36.8 %copy-start.3 = (s32[16]{0:T(128)S(1)}, s32[16]{0:T(128)}, u32[]{:S(2)}) copy-start(s32[16]{0:T(128)} %tail_ref.1) | copy-start | bytes 196
  75.8 22.4 %copy-start = (bf16[16,128,256]{2,1,0:T(8,128)(2,1)}, bf16[16,128,256]{2,1,0:T(8,128)(2,1)S(1)}, u32[]{:S(2)}) copy-start(bf16[16,128,256]{2,1,0:T(8,128)(2,1)S(1)} %all-to-all-done.own_ref) | copy-start | bytes 3145732
  75.8 32.5 %all-to-all-start.1 = ((bf16[32,48,256]{2,1,0:T(8,128)(2,1)}), bf16[32,48,256]{2,1,0:T(8,128)(2,1)S(1)}, u32[]{:S(2)}, u32[]{:S(2)}) async-start(bf16[32,48,256]{2,1,0:T(8,128)(2,1)} %project.1), calls=%async_computation.1 | async-start | bytes 1572864 | tf_op jit(solution)/shard_map/all_to_all | solution.py:344
  87.7 31.4 %collective-permute-start = (bf16[16,128,256]{2,1,0:T(8,128)(2,1)S(1)}, bf16[16,128,256]{2,1,0:T(8,128)(2,1)S(1)}, u32[]{:S(2)}, u32[]{:S(2)}) collective-permute-start(bf16[16,128,256]{2,1,0:T(8,128)(2,1)S(1)} %all-to-all-done.own_ref), channel_id=1, source_target_pairs={{0,1},{1,0},{2,3},{3,2},{4,5},{5,4},{6,7},{7,6},{8,9},{9,8},{10,11... | collective-permute-start | bytes 3145736 | tf_op jit(solution)/shard_map/ppermute | solution.py:377
  108.3 0.9 copy-start.1
  119.1 1.0 copy-start.2

commit v2 on v1

v2 whole, which is shorter than its diff:
```python
import functools
import math

import jax
import jax.numpy as jnp
from jax import lax
from jax.experimental import pallas as pl
from jax.experimental.pallas import tpu as pltpu
from jax.sharding import Mesh, PartitionSpec as P

F32 = jnp.float32
BF16 = jnp.bfloat16
NT = (((1,), (1,)), ((), ()))
LOW = -1e30
VMEM_LIMIT = 56 * 2**20
QUAD = ("xl", "core")
COMP = ("y", "xl", "core")
POOL = ("xh", "z")
SWAP = [(0, 1), (1, 0)]
SMEM = pl.BlockSpec(memory_space=pltpu.SMEM)
VMEM = pl.BlockSpec(memory_space=pltpu.VMEM)


def params():
    return pltpu.CompilerParams(vmem_limit_bytes=VMEM_LIMIT)


def pack_kernel(tail_ref, holder_ref, slot_ref, store_ref, out_ref, index_vmem, index_smem, staged, sem, in_sems, out_sems):
    sessions, cells = holder_ref.shape
    rows = store_ref.shape[1]
    share = out_ref.shape[1] // rows
    me = lax.axis_index("xh") * lax.axis_size("z") + lax.axis_index("z")
    core = lax.axis_index("core")
    row = lax.broadcasted_iota(jnp.int32, (sessions, cells), 0)
    cell = lax.broadcasted_iota(jnp.int32, (sessions, cells), 1)
    tails = jnp.zeros((sessions, cells), jnp.int32)
    for s in range(sessions):
        tails = jnp.where(row == s, tail_ref[s], tails)
    held = (holder_ref[...] == me) & (cell < tails)
    before = lax.broadcasted_iota(jnp.int32, (cells, cells), 0)
    until = lax.broadcasted_iota(jnp.int32, (cells, cells), 1)
    order = jnp.dot(
        jnp.where(held, 1.0, 0.0).astype(BF16),
        jnp.where(before <= until, 1.0, 0.0).astype(BF16),
        preferred_element_type=F32,
    )
    lane = lax.broadcasted_iota(jnp.int32, (sessions, 128), 1)
    packed = jnp.zeros((sessions, 128), jnp.int32)
    for k in range(share):
        wanted = (core * share + k + 1).astype(F32)
        pick = jnp.where(held & (order == wanted), slot_ref[...], 0)
        packed = jnp.where(lane == k, jnp.sum(pick, axis=1, keepdims=True), packed)
    index_vmem[...] = packed
    copy = pltpu.make_async_copy(index_vmem, index_smem, sem)
    copy.start()
    copy.wait()

    def block_in(s, k):
        return pltpu.make_async_copy(
            store_ref.at[index_smem[s, k]], staged.at[s, pl.ds(k * rows, rows)], in_sems.at[s * share + k]
        )

    def slab_out(s):
        return pltpu.make_async_copy(staged.at[s], out_ref.at[s], out_sems.at[s])

    for s in range(sessions):
        for k in range(share):
            block_in(s, k).start()
    for s in range(sessions):
        for k in range(share):
            block_in(s, k).wait()
        slab_out(s).start()
    for s in range(sessions):
        slab_out(s).wait()


def pack_blocks(tail_counts, holder_list, slot_list, store, share):
    sessions, cells = holder_list.shape
    _, rows, width = store.shape
    return pl.pallas_call(
        pack_kernel,
        out_shape=jax.ShapeDtypeStruct((sessions, share * rows, width), store.dtype),
        in_specs=[SMEM, VMEM, VMEM, pl.BlockSpec(memory_space=pl.ANY)],
        out_specs=pl.BlockSpec(memory_space=pl.ANY),
        scratch_shapes=[
            pltpu.VMEM((sessions, 128), jnp.int32),
            pltpu.SMEM((sessions, 128), jnp.int32),
            pltpu.VMEM((sessions, share * rows, width), store.dtype),
            pltpu.SemaphoreType.DMA(()),
            pltpu.SemaphoreType.DMA((sessions * share,)),
            pltpu.SemaphoreType.DMA((sessions,)),
        ],
        compiler_params=params(),
        name="pack_blocks",
    )(tail_counts, holder_list, slot_list, store)


EXTRA = 16


def split_squares(total, rows):
    half = total.shape[1] // 2
    return total[:rows], total[rows:, :half] + total[rows:, half:]


def in_bfloat16(total, rows):
    main, squares = split_squares(total, rows)
    high = squares.astype(BF16)
    low = (squares - high.astype(F32)).astype(BF16)
    return jnp.concatenate([main.astype(BF16), jnp.concatenate([high, low], axis=1)], axis=0)


def block_counts(tail_ref, holder_ref, counts_ref):
    cells = holder_ref.shape[1]
    holders = counts_ref.shape[0]
    session = lax.axis_index("xh") * lax.axis_size("z") + lax.axis_index("z")
    holder = lax.broadcasted_iota(jnp.int32, (holders, cells), 0)
    cell = lax.broadcasted_iota(jnp.int32, (holders, cells), 1)
    match = (holder_ref[pl.ds(session, 1), :] == holder) & (cell < tail_ref[session])
    found = jnp.sum(jnp.where(match, 1.0, 0.0), axis=1, keepdims=True).astype(jnp.int32)
    ids = lax.broadcasted_iota(jnp.int32, (holders, 1), 0)
    full = jnp.max(jnp.where(found >= cells // holders, ids, 0).astype(F32), axis=0, keepdims=True)
    lane = lax.broadcasted_iota(jnp.int32, counts_ref.shape, 1)
    counts = jnp.where(lane == 0, found, 0)
    counts = jnp.where(lane == 1, full.astype(jnp.int32), counts)
    counts_ref[...] = jnp.where(lane == 2, lax.axis_index("core"), counts)


def project_kernel(tail_ref, holder_ref, hidden_ref, gain_ref, weight_ref, send_ref, keep_ref, counts_ref):
    hidden = hidden_ref[...].astype(F32)
    rows = hidden.shape[0]
    width = send_ref.shape[2]
    core = lax.axis_index("core")
    scaled = (hidden * gain_ref[...].astype(F32)).astype(BF16)
    squares = lax.dot_general(
        jnp.ones((EXTRA, hidden.shape[1]), F32), hidden * hidden, NT,
        precision=lax.Precision.HIGHEST, preferred_element_type=F32,
    )
    tail = jnp.concatenate([squares, jnp.zeros_like(squares)], axis=1)
    for out_ref, side in ((send_ref, 1 - core), (keep_ref, core)):
        for x in range(2):
            for j in range(2):
                start = pl.multiple_of((4 * x + 2 * side + j) * width, width)
                out_ref[2 * x + j, :rows, :] = jnp.dot(
                    scaled, weight_ref[:, pl.ds(start, width)], preferred_element_type=F32
                )
                out_ref[2 * x + j, rows:, :] = tail
    block_counts(tail_ref, holder_ref, counts_ref)


def project(tail_counts, holder_list, hidden, gain, weight, heads, holders):
    rows = hidden.shape[0]
    out = jax.ShapeDtypeStruct((heads // 2, rows + EXTRA, weight.shape[1] // heads), F32)
    return pl.pallas_call(
        project_kernel,
        out_shape=(out, out, jax.ShapeDtypeStruct((holders, 128), jnp.int32)),
        in_specs=[SMEM, VMEM, VMEM, VMEM, VMEM],
        compiler_params=params(),
        name="project",
    )(tail_counts, holder_list, hidden, gain, weight)


def join_cores_kernel(recv_ref, mine_ref, *out_refs):
    rows = recv_ref.shape[1] - EXTRA
    turn = lax.rem(lax.axis_index("y"), 4)
    for t, out_ref in enumerate(out_refs):
        head = t ^ turn
        out_ref[...] = in_bfloat16(recv_ref[head] + mine_ref[head], rows)


def join_cores(received, mine):
    out = jax.ShapeDtypeStruct(received.shape[1:], BF16)
    return pl.pallas_call(
        join_cores_kernel, out_shape=(out,) * received.shape[0], compiler_params=params(), name="join_cores"
    )(received, mine)


def join_chips_kernel(*refs):
    total = refs[0][...].astype(F32)
    for ref in refs[1:-1]:
        total = total + ref[...].astype(F32)
    refs[-1][...] = in_bfloat16(total, total.shape[0] - EXTRA)


def join_chips(arrived):
    return pl.pallas_call(
        join_chips_kernel,
        out_shape=jax.ShapeDtypeStruct(arrived[0].shape, BF16),
        compiler_params=params(),
        name="join_chips",
    )(*arrived)


def owners_of_turn(turn):
    pairs = []
    for y in range(8):
        for xl in range(2):
            for core in range(2):
                head = turn ^ (y % 4)
                owner = 4 * (head // 2) + 2 * core + head % 2
                pairs.append((y * 4 + xl * 2 + core, owner * 4 + xl * 2 + y // 4))
    return pairs


def head_sums(tail_counts, holder_list, hidden, gain, weight, heads, holders):
    send, keep, counts = project(tail_counts, holder_list, hidden, gain, weight, heads, holders)
    turns = join_cores(lax.ppermute(send, "core", SWAP), keep)
    arrived = [lax.ppermute(turn, COMP, owners_of_turn(t)) for t, turn in enumerate(turns)]
    return counts, arrived


def rotation(rows, head_dim):
    positions = jnp.arange(rows, dtype=jnp.int32).astype(F32)
    frequency = 500000.0 ** (-2.0 * jnp.arange(head_dim // 2, dtype=F32) / head_dim)
    angles = positions[:, None] * frequency[None, :]
    cosine = jnp.cos(angles)
    sine = jnp.sin(angles)
    return jnp.concatenate([cosine, cosine], axis=1), jnp.concatenate([-sine, sine], axis=1)


def finish_head(width_total, gathered_ref, cos_ref, sin_ref):
    rows = gathered_ref.shape[1] - EXTRA
    half = gathered_ref.shape[2] // 2
    total = gathered_ref[0].astype(F32)
    for i in range(1, gathered_ref.shape[0]):
        total = total + gathered_ref[i].astype(F32)
    main, squares = split_squares(total, rows)
    lane = lax.broadcasted_iota(jnp.int32, (rows, half), 1)
    row = lax.broadcasted_iota(jnp.int32, (rows, half), 0)
    squares = jnp.sum(jnp.where(lane == row, squares[:1], 0.0), axis=1, keepdims=True)
    block = main * lax.rsqrt(squares / width_total + 1e-05)
    keys = block[:, :half]
    swapped = jnp.concatenate([keys[:, half // 2 :], keys[:, : half // 2]], axis=1)
    return keys * cos_ref[...] + swapped * sin_ref[...], block[:, half:]


def scaled_queries(queries, head_dim):
    scaled = queries.astype(F32) * (math.log2(math.e) / math.sqrt(head_dim))
    high = scaled.astype(BF16)
    low = (scaled - high.astype(F32)).astype(BF16)
    return jnp.concatenate([high, low], axis=1)


def extend(state, query, keys, values, mask=None):
    scores = lax.dot_general(query, keys, NT, preferred_element_type=F32)
    if mask is not None:
        scores = jnp.where(mask, scores, LOW)
    peak = jnp.max(scores, axis=1, keepdims=True)
    if state is not None:
        peak = jnp.maximum(peak, state[0])
    mixed = jnp.dot(jnp.exp2(scores - peak).astype(BF16), values, preferred_element_type=F32)
    if state is not None:
        mixed = mixed + state[1] * jnp.exp2(state[0] - peak)
    return peak, mixed


def attend_kernel(block, chunk, width_total, counts_ref, split_ref, queries_ref, fresh_ref, own_ref, other_ref,
                  gathered_ref, cos_ref, sin_ref, out_ref, blocks, live, sems):
    holders, slab, width = own_ref.shape
    head_dim = width // 2
    head_rows = gathered_ref.shape[1] - EXTRA
    loaded_rows = 2 * holders * slab
    share = 2
    rows = slab // share
    full = counts_ref[0, 1]
    core = counts_ref[0, 2]
    copies = [
        pltpu.make_async_copy(ref, blocks.at[pl.ds(side * holders, holders)], sems.at[side])
        for side, ref in enumerate((own_ref, other_ref))
    ]
    for copy in copies:
        copy.start()
    live[...] = jnp.ones(live.shape, BF16)

    def gather_blocks():
        for copy in copies:
            copy.wait()

        def mend(holder, _):
            for side in range(2):
                for k in range(share):

                    @pl.when((core if side == 0 else 1 - core) * share + k >= counts_ref[holder, 0])
                    def _():
                        here = pl.ds(k * rows, rows)
                        place = side * holders + holder
                        spare = side * holders + full
                        blocks[place, here, :head_dim] = blocks[spare, here, :head_dim]
                        blocks[place, here, head_dim:] = jnp.zeros((rows, head_dim), BF16)
                        live[place, here, :] = jnp.zeros((rows, head_dim), BF16)

            return 0

        lax.fori_loop(0, holders, mend, 0)
        position = lax.broadcasted_iota(jnp.int32, (head_rows, head_dim), 0)
        admitted = position < split_ref[0] * rows
        keys, values = finish_head(width_total, gathered_ref, cos_ref, sin_ref)
        spare = blocks[full, :16, :head_dim].astype(F32)[:1]
        blocks[2 * holders, :head_rows, :head_dim] = jnp.where(admitted, keys, spare).astype(BF16)
        blocks[2 * holders, :head_rows, head_dim:] = jnp.where(admitted, values, 0.0).astype(BF16)
        live[2 * holders, :head_rows, :] = jnp.where(admitted, 1.0, 0.0).astype(BF16)

    heads = queries_ref.shape[1] // head_dim
    total_rows = queries_ref.shape[0]
    row = lax.broadcasted_iota(jnp.int32, (block, block), 0)
    column = lax.broadcasted_iota(jnp.int32, (block, block), 1)
    step = chunk // slab
    starts = list(range(0, 2 * holders, step))

    def doubled(keys):
        return jnp.concatenate([keys, keys], axis=1)

    for b in range(total_rows // block):
        here = pl.ds(b * block, block)
        query = [
            scaled_queries(queries_ref[here, h * head_dim : (h + 1) * head_dim], head_dim) for h in range(heads)
        ]
        state = [None] * heads
        for earlier in range(b + 1):
            there = pl.ds(earlier * block, block)
            keys = doubled(fresh_ref[there, :head_dim])
            values = fresh_ref[there, head_dim:]
            values = jnp.concatenate([values, jnp.ones_like(values)], axis=1)
            for h in range(heads):
                mask = column <= row if earlier == b else None
                state[h] = extend(state[h], query[h], keys, values, mask)
        if b == 0:
            gather_blocks()
        for start in starts:
            parts = list(range(start, start + step))
            taken = [blocks[i] for i in parts]
            weights = [live[i] for i in parts]
            if start == starts[-1]:
                taken.append(blocks[2 * holders, :head_rows])
                weights.append(live[2 * holders, :head_rows])
            taken = jnp.concatenate(taken, axis=0)
            values = jnp.concatenate([taken[:, head_dim:], jnp.concatenate(weights, axis=0)], axis=1)
            for h in range(heads):
                state[h] = extend(state[h], query[h], doubled(taken[:, :head_dim]), values)
        for h in range(heads):
            mixed = state[h][1]
            out_ref[here, h * head_dim : (h + 1) * head_dim] = (
                mixed[:, :head_dim] / mixed[:, head_dim:]
            ).astype(BF16)


def attend(counts, split, queries, fresh, own, other, gathered, width_total):
    rows, width = queries.shape
    holders, slab, pair = own.shape
    cosine, sine = rotation(gathered.shape[1] - EXTRA, pair // 2)
    anywhere = pl.BlockSpec(memory_space=pl.ANY)
    return pl.pallas_call(
        functools.partial(attend_kernel, min(512, rows), 512, width_total),
        in_specs=[SMEM, SMEM, VMEM, VMEM, anywhere, anywhere, VMEM, VMEM, VMEM],
        out_specs=VMEM,
        scratch_shapes=[
            pltpu.VMEM((2 * holders + 1, slab, pair), BF16),
            pltpu.VMEM((2 * holders + 1, slab, pair // 2), BF16),
            pltpu.SemaphoreType.DMA((2,)),
        ],
        out_shape=jax.ShapeDtypeStruct((rows, width), BF16),
        compiler_params=params(),
        cost_estimate=pl.CostEstimate(flops=2**34, bytes_accessed=2**22, transcendentals=2**23),
        name="attend",
    )(counts, split, queries, fresh, own, other, gathered, cosine, sine)


def per_device(
    queries,
    fresh_kv,
    head_hidden,
    norm_gain,
    kv_weight,
    kv_store,
    split_blocks,
    tail_counts,
    holder_list,
    slot_list,
):
    holders = lax.axis_size(POOL)
    capacity = holder_list.shape[1] // holders
    outgoing = pack_blocks(tail_counts, holder_list, slot_list, kv_store[:, :, 0, :], capacity // 2)
    own = lax.all_to_all(outgoing, POOL, split_axis=0, concat_axis=0, tiled=True)
    counts, arrived = head_sums(
        tail_counts, holder_list, head_hidden[0], norm_gain[None, :], kv_weight, lax.axis_size("y"), holders
    )
    own, arrived = lax.optimization_barrier((own, arrived))
    other = lax.ppermute(own, "core", SWAP)
    gathered = lax.all_gather(join_chips(arrived), QUAD, axis=0)
    return attend(
        counts,
        split_blocks,
        queries[0],
        fresh_kv[0, :, 0, :],
        own,
        other,
        gathered,
        head_hidden.shape[2] * lax.axis_size(COMP),
    )[None]


def solution(mesh):
    fine = Mesh(mesh.devices.reshape(2, 8, 8, 2, 2), ("xh", "z", "y", "xl", "core"))
    return jax.shard_map(
        per_device,
        mesh=fine,
        in_specs=(
            P(POOL, None, COMP),
            P(POOL, None, COMP, None),
            P(POOL, None, COMP),
            P(COMP),
            P(COMP, None),
            P(POOL, None, COMP, None),
            P(POOL),
            P(),
            P(),
            P(),
        ),
        out_specs=P(POOL, None, COMP),
        check_vma=False,
    )
```

time: 142 us -> 82.2 us (0.58)
  Pallas kernels: 65.7 us -> 27 us
  waiting for transfers between devices: 33.9 us -> 7.13 us
  starting transfers between devices: 25.5 us -> 35.3 us
  other arithmetic: 4.21 us -> 1.08 us
    pallas_call x1, Pallas kernels: 34.9 us -> 4.35 us  [pack_blocks(): pl.pallas_call(pack_kernel, out_shape=jax.ShapeDtypeStruct((sessions, sha...]
    all_to_all x1, waiting for transfers between devices: 23.8 us -> 0.01 us  [per_device(): lax.all_to_all(outgoing, POOL, split_axis=0, concat_axis=0, tiled=True)]
    ppermute x1 -> x6, starting transfers between devices: 2.14 us -> 21.8 us  [the longest x4 16.9 us: head_sums(): lax.ppermute(turn, COMP, owners_of_turn(t))]
    all_to_all x1 -> x0, waiting for transfers between devices: 10.1 us -> none  [per_device(): lax.all_to_all(partial_sums, COMP, split_axis=0, concat_axis=0, tiled=True)]
    all_to_all x1 -> x0, starting transfers between devices: 9.88 us -> none  [per_device(): lax.all_to_all(partial_sums, COMP, split_axis=0, concat_axis=0, tiled=True)]
    pallas_call x4, Pallas kernels: 30.8 us -> 22.6 us  [the longest x1 16.3 us: attend(): pl.pallas_call(functools.partial(attend_kernel, min(512, rows), 512, widt...]
    ppermute x1 -> x6, waiting for transfers between devices: 0.01 us -> 7.13 us  [the longest x4 5.31 us: head_sums(): lax.ppermute(turn, COMP, owners_of_turn(t))]
  transfers between devices with their start and end apart: 3 -> 7, of which waited for: 2 -> 3; matrix products, arithmetic and copies ran while one was open for 4% -> 2% of each run, Pallas kernels for 7% -> 8%
where the time goes in v2:
time: 82.2 us; the launch traced here: 80.9 us
  starting transfers between devices  35.3 us (43%)
  Pallas kernels  27 us (33%)
  waiting for transfers between devices  7.13 us (9%)
  blocking collectives  7.02 us (9%)
  local copies, waits for them, and re-layouts  2.38 us (3%)
  other arithmetic  1.08 us (1%)
  between operations  0.95 us (1%)
    ppermute x4, starting transfers between devices, head_sums(): lax.ppermute(turn, COMP, owners_of_turn(t))  16.9 us
    pallas_call x1, Pallas kernels, attend(): pl.pallas_call(functools.partial(attend_kernel, min(512, rows), 512, widt...  16.3 us
    all_to_all x1, starting transfers between devices, per_device(): lax.all_to_all(outgoing, POOL, split_axis=0, concat_axis=0, tiled=True)  13.6 us
    all_gather x1, blocking collectives, per_device(): gathered = lax.all_gather(join_chips(arrived), QUAD, axis=0)  7.02 us
    ppermute x4, waiting for transfers between devices, head_sums(): lax.ppermute(turn, COMP, owners_of_turn(t))  5.31 us
    pallas_call x1, Pallas kernels, pack_blocks(): pl.pallas_call(pack_kernel, out_shape=jax.ShapeDtypeStruct((sessions, sha...  4.35 us
    pallas_call x1, Pallas kernels, project(): pl.pallas_call(project_kernel, out_shape=(out, out, jax.ShapeDtypeStruct(...  2.67 us
    ppermute x1, starting transfers between devices, head_sums(): turns = join_cores(lax.ppermute(send, 'core', SWAP), keep)  2.52 us
  transfers between devices with their start and end apart: 7, of which 3 were waited for; matrix products, arithmetic and copies ran while one was open for 2% of the time, Pallas kernels for 8%

profile of v2, /device:TPU:1, one launch (start us, length us, event | category | flops | bytes accessed | tf_op | source)
XLA Modules:
  0.0 80.9 jit_solution(14261762214948886188)
XLA Ops:
  0.0 0.0 copy-start.7
  0.0 4.3 %pack_blocks.1 = bf16[16,128,256]{2,1,0:T(8,128)(2,1)} custom-call(s32[16]{0:T(128)} %tail_ref.3, s32[16,64]{1,0:T(8,128)} %holder_ref.3, s32[16,64]{1,0:T(8,128)} %slot_ref.1, bf16[64,64,256]{2,1,0:T(8,128)(2,1)} %bitcast.6), custom_call_target="tpu_custom_call" | custom-call | tf_op jit(solution)/shard_map/pack_blocks/pallas_call | solution.py:80
  4.4 13.6 %all-to-all-start = ((bf16[16,128,256]{2,1,0:T(8,128)(2,1)}), bf16[16,128,256]{2,1,0:T(8,128)(2,1)S(1)}, u32[]{:S(2)}, u32[]{:S(2)}) async-start(bf16[16,128,256]{2,1,0:T(8,128)(2,1)} %pack_blocks.1), calls=%async_computation | async-start | bytes 2097152 | tf_op jit(solution)/shard_map/all_to_all | solution.py:383
  17.9 0.0 copy-done.7
  17.9 0.6 broadcast_in_dim.8.gain_ref
  18.5 2.7 %project.1 = (f32[4,144,256]{2,1,0:T(8,128)}, f32[4,144,256]{2,1,0:T(8,128)}, s32[16,128]{1,0:T(8,128)}) custom-call(s32[16]{0:T(128)} %tail_ref.3, s32[16,64]{1,0:T(8,128)} %holder_ref.3, bf16[128,256]{1,0:T(8,128)(2,1)} %bitcast.8, bf16[1,256]{1,0:T(2,128)(2,1)} %broadcast_in_dim.8.gain_ref, bf16[256,2048]{1,0:T(8,128)(2,1)} %weight_ref.1), custom_call_target="tpu_custom_call" | custom-call | tf_op jit(solution)/shard_map/project/pallas_call | solution.py:154
  21.2 2.5 %collective-permute-start = (f32[4,144,256]{2,1,0:T(8,128)}, f32[4,144,256]{2,1,0:T(8,128)S(1)}, u32[]{:S(2)}, u32[]{:S(2)}) collective-permute-start(f32[4,144,256]{2,1,0:T(8,128)} %get-tuple-element.18), channel_id=1, source_target_pairs={{0,1},{1,0},{2,3},{3,2},{4,5},{5,4},{6,7},{7,6},{8,9},{9,8},{10,11... | collective-permute-start | bytes 1769480 | tf_op jit(solution)/shard_map/ppermute | solution.py:207
  23.7 1.8 %collective-permute-done.recv_ref = f32[4,144,256]{2,1,0:T(8,128)S(1)} collective-permute-done((f32[4,144,256]{2,1,0:T(8,128)}, f32[4,144,256]{2,1,0:T(8,128)S(1)}, u32[]{:S(2)}, u32[]{:S(2)}) %collective-permute-start) | collective-permute-done | bytes 589856 | tf_op jit(solution)/shard_map/ppermute | solution.py:207
  25.5 0.0 copy-start.1
  25.5 0.8 copy-done.1
  26.3 2.0 %join_cores.1 = (bf16[144,256]{1,0:T(8,128)(2,1)}, bf16[144,256]{1,0:T(8,128)(2,1)}, bf16[144,256]{1,0:T(8,128)(2,1)}, bf16[144,256]{1,0:T(8,128)(2,1)}) custom-call(f32[4,144,256]{2,1,0:T(8,128)} %copy-done.1, f32[4,144,256]{2,1,0:T(8,128)} %get-tuple-element.19.mine_ref), custom_call_target="tpu_custom_call" | custom-call | tf_op jit(solution)/shard_map/join_cores/pallas_call | solution.py:173
  28.3 4.5 %collective-permute-start.1 = (bf16[144,256]{1,0:T(8,128)(2,1)}, bf16[144,256]{1,0:T(8,128)(2,1)S(1)}, u32[]{:S(2)}, u32[]{:S(2)}) collective-permute-start(bf16[144,256]{1,0:T(8,128)(2,1)} %get-tuple-element.20), channel_id=1, source_target_pairs={{0,0},{1,8},{2,2},{3,10},{4,4},{5,12},{6,6},{7,14},{8,16},{9,24},{... | collective-permute-start | bytes 221192 | tf_op jit(solution)/shard_map/ppermute | solution.py:208
  32.8 5.8 %collective-permute-start.2 = (bf16[144,256]{1,0:T(8,128)(2,1)}, bf16[144,256]{1,0:T(8,128)(2,1)S(1)}, u32[]{:S(2)}, u32[]{:S(2)}) collective-permute-start(bf16[144,256]{1,0:T(8,128)(2,1)} %get-tuple-element.21), channel_id=1, source_target_pairs={{0,4},{1,12},{2,6},{3,14},{4,0},{5,8},{6,2},{7,10},{8,20},{9,28},{... | collective-permute-start | bytes 221192 | tf_op jit(solution)/shard_map/ppermute | solution.py:208
  38.6 1.9 %collective-permute-start.3 = (bf16[144,256]{1,0:T(8,128)(2,1)}, bf16[144,256]{1,0:T(8,128)(2,1)S(1)}, u32[]{:S(2)}, u32[]{:S(2)}) collective-permute-start(bf16[144,256]{1,0:T(8,128)(2,1)} %get-tuple-element.22), channel_id=1, source_target_pairs={{0,16},{1,24},{2,18},{3,26},{4,20},{5,28},{6,22},{7,30},{8,0},{9,8... | collective-permute-start | bytes 221192 | tf_op jit(solution)/shard_map/ppermute | solution.py:208
  40.6 4.7 %collective-permute-start.4 = (bf16[144,256]{1,0:T(8,128)(2,1)}, bf16[144,256]{1,0:T(8,128)(2,1)S(1)}, u32[]{:S(2)}, u32[]{:S(2)}) collective-permute-start(bf16[144,256]{1,0:T(8,128)(2,1)} %get-tuple-element.23), channel_id=1, source_target_pairs={{0,20},{1,28},{2,22},{3,30},{4,16},{5,24},{6,18},{7,26},{8,4},{9,1... | collective-permute-start | bytes 221192 | tf_op jit(solution)/shard_map/ppermute | solution.py:208
  45.3 0.0 collective-permute-done.1.refs_0_
  45.3 0.0 copy-start.2
  45.3 0.0 collective-permute-done.2.refs_1_
  45.3 0.0 copy-start.3
  45.3 2.8 %collective-permute-done.3.refs_2_ = bf16[144,256]{1,0:T(8,128)(2,1)S(1)} collective-permute-done((bf16[144,256]{1,0:T(8,128)(2,1)}, bf16[144,256]{1,0:T(8,128)(2,1)S(1)}, u32[]{:S(2)}, u32[]{:S(2)}) %collective-permute-start.3) | collective-permute-done | bytes 73760 | tf_op jit(solution)/shard_map/ppermute | solution.py:208
  48.1 0.0 copy-start.4
  48.1 2.5 %collective-permute-done.4.refs_3_ = bf16[144,256]{1,0:T(8,128)(2,1)S(1)} collective-permute-done((bf16[144,256]{1,0:T(8,128)(2,1)}, bf16[144,256]{1,0:T(8,128)(2,1)S(1)}, u32[]{:S(2)}, u32[]{:S(2)}) %collective-permute-start.4) | collective-permute-done | bytes 73760 | tf_op jit(solution)/shard_map/ppermute | solution.py:208
  50.6 0.0 copy-start.5
  50.7 0.0 all-to-all-done.own_ref
  50.7 0.0 copy-start
  50.7 2.3 %collective-permute-start.5 = (bf16[16,128,256]{2,1,0:T(8,128)(2,1)S(1)}, bf16[16,128,256]{2,1,0:T(8,128)(2,1)S(1)}, u32[]{:S(2)}, u32[]{:S(2)}) collective-permute-start(bf16[16,128,256]{2,1,0:T(8,128)(2,1)S(1)} %all-to-all-done.own_ref), channel_id=1, source_target_pairs={{0,1},{1,0},{2,3},{3,2},{4,5},{5,4},{6,7},{7,6},{8,9},{9,8},{10,11... | collective-permute-start | bytes 3145736 | tf_op jit(solution)/shard_map/ppermute | solution.py:388
  53.6 0.3 fusion
  54.0 0.8 pad_maximum_fusion
  54.7 0.0 copy-done.2
  54.7 0.0 copy-done.3
  54.7 0.0 copy-done.4
  54.7 0.0 copy-done.5
  54.7 1.7 %join_chips.1 = bf16[144,256]{1,0:T(8,128)(2,1)} custom-call(bf16[144,256]{1,0:T(8,128)(2,1)} %copy-done.2, bf16[144,256]{1,0:T(8,128)(2,1)} %copy-done.3, bf16[144,256]{1,0:T(8,128)(2,1)} %copy-done.4, bf16[144,256]{1,0:T(8,128)(2,1)} %copy-done.5), custom_call_target="tpu_custom_call" | custom-call | tf_op jit(solution)/shard_map/join_chips/pallas_call | solution.py:186
  56.4 7.0 %all-gather = bf16[576,256]{1,0:T(8,128)(2,1)} all-gather(bf16[144,256]{1,0:T(8,128)(2,1)} %join_chips.1), channel_id=2, replica_groups=mesh['xh'=2,'z'=8,'y'=8,'xl'=2,'core'=2] {'xl','core'}, dimensions={0}, use_global_device_ids=true | all-gather | bytes 368640 | tf_op jit(solution)/shard_map/all_gather | solution.py:389
  63.4 0.0 collective-permute-done.5.other_ref
  63.4 0.0 copy-start.6
  63.4 0.0 copy-done
  63.4 1.0 %copy-done.6 = bf16[16,128,256]{2,1,0:T(8,128)(2,1)} copy-done((bf16[16,128,256]{2,1,0:T(8,128)(2,1)}, bf16[16,128,256]{2,1,0:T(8,128)(2,1)S(1)}, u32[]{:S(2)}) %copy-start.6) | copy-done | bytes 1048600
  64.4 16.3 %attend.1 = bf16[1024,256]{1,0:T(8,128)(2,1)} custom-call(s32[16,128]{1,0:T(8,128)} %get-tuple-element.17.counts_ref, s32[1]{0:T(128)S(6)} %copy.11.split_ref, bf16[1024,256]{1,0:T(8,128)(2,1)} %bitcast.9, bf16[1024,256]{1,0:T(8,128)(2,1)} %bitcast.10, bf16[16,128,256]{2,1,0:T(8,128)(2,1)} %copy-done, bf16[16,128,256]{2,1,0:T(8,128)(2,1)} %copy-done.6, ...), custom_call_target="tpu_custom_call" | custom-call | flops 17179869184 | bytes 4194304 | tf_op jit(solution)/shard_map/attend/pallas_call | solution.py:352
  (2 shorter events, 0.0 us)
Async XLA Ops:
  0.0 17.9 %copy-start.7 = (bf16[256]{0:T(256)(128)(2,1)S(1)}, bf16[256]{0:T(256)(128)(2,1)}, u32[]{:S(2)}) copy-start(bf16[256]{0:T(256)(128)(2,1)} %param.13) | copy-start | bytes 1540
  4.4 46.3 %all-to-all-start = ((bf16[16,128,256]{2,1,0:T(8,128)(2,1)}), bf16[16,128,256]{2,1,0:T(8,128)(2,1)S(1)}, u32[]{:S(2)}, u32[]{:S(2)}) async-start(bf16[16,128,256]{2,1,0:T(8,128)(2,1)} %pack_blocks.1), calls=%async_computation | async-start | bytes 2097152 | tf_op jit(solution)/shard_map/all_to_all | solution.py:383
  21.2 4.4 %collective-permute-start = (f32[4,144,256]{2,1,0:T(8,128)}, f32[4,144,256]{2,1,0:T(8,128)S(1)}, u32[]{:S(2)}, u32[]{:S(2)}) collective-permute-start(f32[4,144,256]{2,1,0:T(8,128)} %get-tuple-element.18), channel_id=1, source_target_pairs={{0,1},{1,0},{2,3},{3,2},{4,5},{5,4},{6,7},{7,6},{8,9},{9,8},{10,11... | collective-permute-start | bytes 1769480 | tf_op jit(solution)/shard_map/ppermute | solution.py:207
  25.5 0.8 copy-start.1
  28.3 17.0 %collective-permute-start.1 = (bf16[144,256]{1,0:T(8,128)(2,1)}, bf16[144,256]{1,0:T(8,128)(2,1)S(1)}, u32[]{:S(2)}, u32[]{:S(2)}) collective-permute-start(bf16[144,256]{1,0:T(8,128)(2,1)} %get-tuple-element.20), channel_id=1, source_target_pairs={{0,0},{1,8},{2,2},{3,10},{4,4},{5,12},{6,6},{7,14},{8,16},{9,24},{... | collective-permute-start | bytes 221192 | tf_op jit(solution)/shard_map/ppermute | solution.py:208
  32.8 12.5 %collective-permute-start.2 = (bf16[144,256]{1,0:T(8,128)(2,1)}, bf16[144,256]{1,0:T(8,128)(2,1)S(1)}, u32[]{:S(2)}, u32[]{:S(2)}) collective-permute-start(bf16[144,256]{1,0:T(8,128)(2,1)} %get-tuple-element.21), channel_id=1, source_target_pairs={{0,4},{1,12},{2,6},{3,14},{4,0},{5,8},{6,2},{7,10},{8,20},{9,28},{... | collective-permute-start | bytes 221192 | tf_op jit(solution)/shard_map/ppermute | solution.py:208
  38.6 9.5 %collective-permute-start.3 = (bf16[144,256]{1,0:T(8,128)(2,1)}, bf16[144,256]{1,0:T(8,128)(2,1)S(1)}, u32[]{:S(2)}, u32[]{:S(2)}) collective-permute-start(bf16[144,256]{1,0:T(8,128)(2,1)} %get-tuple-element.22), channel_id=1, source_target_pairs={{0,16},{1,24},{2,18},{3,26},{4,20},{5,28},{6,22},{7,30},{8,0},{9,8... | collective-permute-start | bytes 221192 | tf_op jit(solution)/shard_map/ppermute | solution.py:208
  40.6 10.1 %collective-permute-start.4 = (bf16[144,256]{1,0:T(8,128)(2,1)}, bf16[144,256]{1,0:T(8,128)(2,1)S(1)}, u32[]{:S(2)}, u32[]{:S(2)}) collective-permute-start(bf16[144,256]{1,0:T(8,128)(2,1)} %get-tuple-element.23), channel_id=1, source_target_pairs={{0,20},{1,28},{2,22},{3,30},{4,16},{5,24},{6,18},{7,26},{8,4},{9,1... | collective-permute-start | bytes 221192 | tf_op jit(solution)/shard_map/ppermute | solution.py:208
  45.3 9.4 %copy-start.2 = (bf16[144,256]{1,0:T(8,128)(2,1)}, bf16[144,256]{1,0:T(8,128)(2,1)S(1)}, u32[]{:S(2)}) copy-start(bf16[144,256]{1,0:T(8,128)(2,1)S(1)} %collective-permute-done.1.refs_0_) | copy-start | bytes 221188
  45.3 9.4 %copy-start.3 = (bf16[144,256]{1,0:T(8,128)(2,1)}, bf16[144,256]{1,0:T(8,128)(2,1)S(1)}, u32[]{:S(2)}) copy-start(bf16[144,256]{1,0:T(8,128)(2,1)S(1)} %collective-permute-done.2.refs_1_) | copy-start | bytes 221188
  48.1 6.6 %copy-start.4 = (bf16[144,256]{1,0:T(8,128)(2,1)}, bf16[144,256]{1,0:T(8,128)(2,1)S(1)}, u32[]{:S(2)}) copy-start(bf16[144,256]{1,0:T(8,128)(2,1)S(1)} %collective-permute-done.3.refs_2_) | copy-start | bytes 221188
  50.6 4.1 %copy-start.5 = (bf16[144,256]{1,0:T(8,128)(2,1)}, bf16[144,256]{1,0:T(8,128)(2,1)S(1)}, u32[]{:S(2)}) copy-start(bf16[144,256]{1,0:T(8,128)(2,1)S(1)} %collective-permute-done.4.refs_3_) | copy-start | bytes 221188
  50.7 12.8 %copy-start = (bf16[16,128,256]{2,1,0:T(8,128)(2,1)}, bf16[16,128,256]{2,1,0:T(8,128)(2,1)S(1)}, u32[]{:S(2)}) copy-start(bf16[16,128,256]{2,1,0:T(8,128)(2,1)S(1)} %all-to-all-done.own_ref) | copy-start | bytes 3145732
  50.7 12.8 %collective-permute-start.5 = (bf16[16,128,256]{2,1,0:T(8,128)(2,1)S(1)}, bf16[16,128,256]{2,1,0:T(8,128)(2,1)S(1)}, u32[]{:S(2)}, u32[]{:S(2)}) collective-permute-start(bf16[16,128,256]{2,1,0:T(8,128)(2,1)S(1)} %all-to-all-done.own_ref), channel_id=1, source_target_pairs={{0,1},{1,0},{2,3},{3,2},{4,5},{5,4},{6,7},{7,6},{8,9},{9,8},{10,11... | collective-permute-start | bytes 3145736 | tf_op jit(solution)/shard_map/ppermute | solution.py:388
  63.4 1.0 %copy-start.6 = (bf16[16,128,256]{2,1,0:T(8,128)(2,1)}, bf16[16,128,256]{2,1,0:T(8,128)(2,1)S(1)}, u32[]{:S(2)}) copy-start(bf16[16,128,256]{2,1,0:T(8,128)(2,1)S(1)} %collective-permute-done.5.other_ref) | copy-start | bytes 3145732

commit v3 on v2

--- a/solution.py
+++ b/solution.py
@@ -3,6 +3,7 @@
 
 import jax
 import jax.numpy as jnp
+import numpy as np
 from jax import lax
 from jax.experimental import pallas as pl
 from jax.experimental.pallas import tpu as pltpu
@@ -12,7 +13,6 @@
 BF16 = jnp.bfloat16
 NT = (((1,), (1,)), ((), ()))
 LOW = -1e30
-VMEM_LIMIT = 56 * 2**20
 QUAD = ("xl", "core")
 COMP = ("y", "xl", "core")
 POOL = ("xh", "z")
@@ -21,14 +21,47 @@
 VMEM = pl.BlockSpec(memory_space=pltpu.VMEM)
 
 
-def params():
-    return pltpu.CompilerParams(vmem_limit_bytes=VMEM_LIMIT)
-
-
-def pack_kernel(tail_ref, holder_ref, slot_ref, store_ref, out_ref, index_vmem, index_smem, staged, sem, in_sems, out_sems):
+def params(mebibytes):
+    return pltpu.CompilerParams(vmem_limit_bytes=mebibytes * 2**20)
+
+
+EXTRA = 16
+
+
+def split_squares(total, rows):
+    half = total.shape[1] // 2
+    return total[:rows], total[rows:, :half] + total[rows:, half:]
+
+
+def in_bfloat16(total, rows):
+    main, squares = split_squares(total, rows)
+    high = squares.astype(BF16)
+    low = (squares - high.astype(F32)).astype(BF16)
+    return jnp.concatenate([main.astype(BF16), jnp.concatenate([high, low], axis=1)], axis=0)
+
+
+def block_counts(tail_ref, holder_ref, counts_ref):
+    cells = holder_ref.shape[1]
+    holders = counts_ref.shape[0]
+    session = lax.axis_index("xh") * lax.axis_size("z") + lax.axis_index("z")
+    holder = lax.broadcasted_iota(jnp.int32, (holders, cells), 0)
+    cell = lax.broadcasted_iota(jnp.int32, (holders, cells), 1)
+    match = (holder_ref[pl.ds(session, 1), :] == holder) & (cell < tail_ref[session])
+    found = jnp.sum(jnp.where(match, 1.0, 0.0), axis=1, keepdims=True).astype(jnp.int32)
+    ids = lax.broadcasted_iota(jnp.int32, (holders, 1), 0)
+    full = jnp.max(jnp.where(found >= cells // holders, ids, 0).astype(F32), axis=0, keepdims=True)
+    lane = lax.broadcasted_iota(jnp.int32, counts_ref.shape, 1)
+    counts = jnp.where(lane == 0, found, 0)
+    counts = jnp.where(lane == 1, full.astype(jnp.int32), counts)
+    counts_ref[...] = jnp.where(lane == 2, lax.axis_index("core"), counts)
+
+
+def offsets(turn):
+    return 3 - turn, turn - 4
+
+
+def held_slots(share, tail_ref, holder_ref, slot_ref):
     sessions, cells = holder_ref.shape
-    rows = store_ref.shape[1]
-    share = out_ref.shape[1] // rows
     me = lax.axis_index("xh") * lax.axis_size("z") + lax.axis_index("z")
     core = lax.axis_index("core")
     row = lax.broadcasted_iota(jnp.int32, (sessions, cells), 0)
@@ -45,134 +78,125 @@
         preferred_element_type=F32,
     )
     lane = lax.broadcasted_iota(jnp.int32, (sessions, 128), 1)
-    packed = jnp.zeros((sessions, 128), jnp.int32)
+    slots = jnp.zeros((sessions, 128), jnp.int32)
     for k in range(share):
         wanted = (core * share + k + 1).astype(F32)
         pick = jnp.where(held & (order == wanted), slot_ref[...], 0)
-        packed = jnp.where(lane == k, jnp.sum(pick, axis=1, keepdims=True), packed)
-    index_vmem[...] = packed
-    copy = pltpu.make_async_copy(index_vmem, index_smem, sem)
-    copy.start()
-    copy.wait()
+        slots = jnp.where(lane == k, jnp.sum(pick, axis=1, keepdims=True), slots)
+    return slots
+
+
+def prepare_kernel(tail_ref, holder_ref, slot_ref, hidden_ref, gain_ref, weight_hbm, store_ref,
+                   packed_ref, send_ref, keep_ref, counts_ref,
+                   index_vmem, index_smem, staged, weight_ref, send, keep, sems, in_sems, out_sems):
+    sessions = holder_ref.shape[0]
+    block_rows = store_ref.shape[1]
+    share = packed_ref.shape[1] // block_rows
+    weight_copy = pltpu.make_async_copy(weight_hbm, weight_ref, sems.at[0])
+    weight_copy.start()
+    index_vmem[...] = held_slots(share, tail_ref, holder_ref, slot_ref)
+    index_copy = pltpu.make_async_copy(index_vmem, index_smem, sems.at[1])
+    index_copy.start()
+    index_copy.wait()
 
     def block_in(s, k):
         return pltpu.make_async_copy(
-            store_ref.at[index_smem[s, k]], staged.at[s, pl.ds(k * rows, rows)], in_sems.at[s * share + k]
+            store_ref.at[index_smem[s, k]],
+            staged.at[s, pl.ds(k * block_rows, block_rows)],
+            in_sems.at[s * share + k],
         )
 
     def slab_out(s):
-        return pltpu.make_async_copy(staged.at[s], out_ref.at[s], out_sems.at[s])
+        return pltpu.make_async_copy(staged.at[s], packed_ref.at[s], out_sems.at[s])
 
     for s in range(sessions):
         for k in range(share):
             block_in(s, k).start()
+
+    hidden = hidden_ref[...].astype(F32)
+    rows = hidden.shape[0]
+    width = send.shape[2]
+    core = lax.axis_index("core")
+    scaled = (hidden * gain_ref[...].astype(F32)[None, :]).astype(BF16)
+    squares = lax.dot_general(
+        jnp.ones((EXTRA, hidden.shape[1]), F32), hidden * hidden, NT,
+        precision=lax.Precision.HIGHEST, preferred_element_type=F32,
+    )
+    weight_copy.wait()
+
+    def partial_sums(t, side):
+        head = lax.rem(lax.axis_index("y") + jnp.where(side == 0, *offsets(t)) + 8, 8)
+        columns = pl.ds(pl.multiple_of(head * width, width), width)
+        return jnp.dot(scaled, weight_ref[:, columns], preferred_element_type=F32)
+
+    high = squares.astype(BF16)
+    low = (squares - high.astype(F32)).astype(BF16)
+    for t in range(4):
+        send[t, :rows, :] = partial_sums(t, 1 - core).astype(BF16)
+        send[t, rows:, :] = jnp.concatenate([high, low], axis=1)
+    send_copy = pltpu.make_async_copy(send, send_ref, sems.at[2])
+    send_copy.start()
+    for t in range(4):
+        keep[t, :rows, :] = partial_sums(t, core)
+        keep[t, rows:, :] = jnp.concatenate([squares, jnp.zeros_like(squares)], axis=1)
+    keep_copy = pltpu.make_async_copy(keep, keep_ref, sems.at[3])
+    keep_copy.start()
+    block_counts(tail_ref, holder_ref, counts_ref)
+
     for s in range(sessions):
         for k in range(share):
             block_in(s, k).wait()
         slab_out(s).start()
+    send_copy.wait()
+    keep_copy.wait()
     for s in range(sessions):
         slab_out(s).wait()
 
 
-def pack_blocks(tail_counts, holder_list, slot_list, store, share):
+def prepare(tail_counts, holder_list, slot_list, hidden, gain, weight, store, share, holders, heads):
     sessions, cells = holder_list.shape
-    _, rows, width = store.shape
+    _, block_rows, width = store.shape
+    partials = (heads // 2, hidden.shape[0] + EXTRA, width)
+    packed = (sessions, share * block_rows, width)
+    anywhere = pl.BlockSpec(memory_space=pl.ANY)
     return pl.pallas_call(
-        pack_kernel,
-        out_shape=jax.ShapeDtypeStruct((sessions, share * rows, width), store.dtype),
-        in_specs=[SMEM, VMEM, VMEM, pl.BlockSpec(memory_space=pl.ANY)],
-        out_specs=pl.BlockSpec(memory_space=pl.ANY),
+        prepare_kernel,
+        out_shape=(
+            jax.ShapeDtypeStruct(packed, BF16),
+            jax.ShapeDtypeStruct(partials, BF16),
+            jax.ShapeDtypeStruct(partials, F32),
+            jax.ShapeDtypeStruct((holders, 128), jnp.int32),
+        ),
+        in_specs=[SMEM, VMEM, VMEM, VMEM, VMEM, anywhere, anywhere],
+        out_specs=(anywhere, anywhere, anywhere, VMEM),
         scratch_shapes=[
             pltpu.VMEM((sessions, 128), jnp.int32),
             pltpu.SMEM((sessions, 128), jnp.int32),
-            pltpu.VMEM((sessions, share * rows, width), store.dtype),
-            pltpu.SemaphoreType.DMA(()),
+            pltpu.VMEM(packed, BF16),
+            pltpu.VMEM(weight.shape, BF16),
+            pltpu.VMEM(partials, BF16),
+            pltpu.VMEM(partials, F32),
+            pltpu.SemaphoreType.DMA((4,)),
             pltpu.SemaphoreType.DMA((sessions * share,)),
             pltpu.SemaphoreType.DMA((sessions,)),
         ],
-        compiler_params=params(),
-        name="pack_blocks",
-    )(tail_counts, holder_list, slot_list, store)
-
-
-EXTRA = 16
-
-
-def split_squares(total, rows):
-    half = total.shape[1] // 2
-    return total[:rows], total[rows:, :half] + total[rows:, half:]
-
-
-def in_bfloat16(total, rows):
-    main, squares = split_squares(total, rows)
-    high = squares.astype(BF16)
-    low = (squares - high.astype(F32)).astype(BF16)
-    return jnp.concatenate([main.astype(BF16), jnp.concatenate([high, low], axis=1)], axis=0)
-
-
-def block_counts(tail_ref, holder_ref, counts_ref):
-    cells = holder_ref.shape[1]
-    holders = counts_ref.shape[0]
-    session = lax.axis_index("xh") * lax.axis_size("z") + lax.axis_index("z")
-    holder = lax.broadcasted_iota(jnp.int32, (holders, cells), 0)
-    cell = lax.broadcasted_iota(jnp.int32, (holders, cells), 1)
-    match = (holder_ref[pl.ds(session, 1), :] == holder) & (cell < tail_ref[session])
-    found = jnp.sum(jnp.where(match, 1.0, 0.0), axis=1, keepdims=True).astype(jnp.int32)
-    ids = lax.broadcasted_iota(jnp.int32, (holders, 1), 0)
-    full = jnp.max(jnp.where(found >= cells // holders, ids, 0).astype(F32), axis=0, keepdims=True)
-    lane = lax.broadcasted_iota(jnp.int32, counts_ref.shape, 1)
-    counts = jnp.where(lane == 0, found, 0)
-    counts = jnp.where(lane == 1, full.astype(jnp.int32), counts)
-    counts_ref[...] = jnp.where(lane == 2, lax.axis_index("core"), counts)
-
-
-def project_kernel(tail_ref, holder_ref, hidden_ref, gain_ref, weight_ref, send_ref, keep_ref, counts_ref):
-    hidden = hidden_ref[...].astype(F32)
-    rows = hidden.shape[0]
-    width = send_ref.shape[2]
-    core = lax.axis_index("core")
-    scaled = (hidden * gain_ref[...].astype(F32)).astype(BF16)
-    squares = lax.dot_general(
-        jnp.ones((EXTRA, hidden.shape[1]), F32), hidden * hidden, NT,
-        precision=lax.Precision.HIGHEST, preferred_element_type=F32,
-    )
-    tail = jnp.concatenate([squares, jnp.zeros_like(squares)], axis=1)
-    for out_ref, side in ((send_ref, 1 - core), (keep_ref, core)):
-        for x in range(2):
-            for j in range(2):
-                start = pl.multiple_of((4 * x + 2 * side + j) * width, width)
-                out_ref[2 * x + j, :rows, :] = jnp.dot(
-                    scaled, weight_ref[:, pl.ds(start, width)], preferred_element_type=F32
-                )
-                out_ref[2 * x + j, rows:, :] = tail
-    block_counts(tail_ref, holder_ref, counts_ref)
-
-
-def project(tail_counts, holder_list, hidden, gain, weight, heads, holders):
-    rows = hidden.shape[0]
-    out = jax.ShapeDtypeStruct((heads // 2, rows + EXTRA, weight.shape[1] // heads), F32)
+        compiler_params=params(56),
+        name="prepare",
+    )(tail_counts, holder_list, slot_list, hidden, gain, weight, store)
+
+
+def join_cores_kernel(sent_ref, mine_ref, *out_refs):
+    rows = mine_ref.shape[1] - EXTRA
+    there = 1 - lax.axis_index("core")
+    for t, out_ref in enumerate(out_refs):
+        out_ref[...] = in_bfloat16(sent_ref[there, t].astype(F32) + mine_ref[t], rows)
+
+
+def join_cores(sent, mine):
+    out = jax.ShapeDtypeStruct(mine.shape[1:], BF16)
     return pl.pallas_call(
-        project_kernel,
-        out_shape=(out, out, jax.ShapeDtypeStruct((holders, 128), jnp.int32)),
-        in_specs=[SMEM, VMEM, VMEM, VMEM, VMEM],
-        compiler_params=params(),
-        name="project",
-    )(tail_counts, holder_list, hidden, gain, weight)
-
-
-def join_cores_kernel(recv_ref, mine_ref, *out_refs):
-    rows = recv_ref.shape[1] - EXTRA
-    turn = lax.rem(lax.axis_index("y"), 4)
-    for t, out_ref in enumerate(out_refs):
-        head = t ^ turn
-        out_ref[...] = in_bfloat16(recv_ref[head] + mine_ref[head], rows)
-
-
-def join_cores(received, mine):
-    out = jax.ShapeDtypeStruct(received.shape[1:], BF16)
-    return pl.pallas_call(
-        join_cores_kernel, out_shape=(out,) * received.shape[0], compiler_params=params(), name="join_cores"
-    )(received, mine)
+        join_cores_kernel, out_shape=(out,) * mine.shape[0], compiler_params=params(6), name="join_cores"
+    )(sent, mine)
 
 
 def join_chips_kernel(*refs):
@@ -186,36 +210,28 @@
     return pl.pallas_call(
         join_chips_kernel,
         out_shape=jax.ShapeDtypeStruct(arrived[0].shape, BF16),
-        compiler_params=params(),
+        compiler_params=params(6),
         name="join_chips",
     )(*arrived)
 
 
 def owners_of_turn(turn):
-    pairs = []
-    for y in range(8):
-        for xl in range(2):
-            for core in range(2):
-                head = turn ^ (y % 4)
-                owner = 4 * (head // 2) + 2 * core + head % 2
-                pairs.append((y * 4 + xl * 2 + core, owner * 4 + xl * 2 + y // 4))
-    return pairs
-
-
-def head_sums(tail_counts, holder_list, hidden, gain, weight, heads, holders):
-    send, keep, counts = project(tail_counts, holder_list, hidden, gain, weight, heads, holders)
-    turns = join_cores(lax.ppermute(send, "core", SWAP), keep)
-    arrived = [lax.ppermute(turn, COMP, owners_of_turn(t)) for t, turn in enumerate(turns)]
-    return counts, arrived
+    return [
+        (y * 4 + 2 * xl + core, (y + offsets(turn)[core]) % 8 * 4 + 2 * xl + core)
+        for y in range(8)
+        for xl in range(2)
+        for core in range(2)
+    ]
 
 
 def rotation(rows, head_dim):
-    positions = jnp.arange(rows, dtype=jnp.int32).astype(F32)
-    frequency = 500000.0 ** (-2.0 * jnp.arange(head_dim // 2, dtype=F32) / head_dim)
-    angles = positions[:, None] * frequency[None, :]
-    cosine = jnp.cos(angles)
-    sine = jnp.sin(angles)
-    return jnp.concatenate([cosine, cosine], axis=1), jnp.concatenate([-sine, sine], axis=1)
+    frequency = 500000.0 ** (-2.0 * np.arange(head_dim // 2) / head_dim)
+    angles = np.arange(rows)[:, None] * frequency[None, :]
+    cosine, sine = np.cos(angles), np.sin(angles)
+    return (
+        jnp.asarray(np.concatenate([cosine, cosine], axis=1), F32),
+        jnp.asarray(np.concatenate([-sine, sine], axis=1), F32),
+    )
 
 
 def finish_head(width_total, gathered_ref, cos_ref, sin_ref):
@@ -359,7 +375,7 @@
             pltpu.SemaphoreType.DMA((2,)),
         ],
         out_shape=jax.ShapeDtypeStruct((rows, width), BF16),
-        compiler_params=params(),
+        compiler_params=params(24),
         cost_estimate=pl.CostEstimate(flops=2**34, bytes_accessed=2**22, transcendentals=2**23),
         name="attend",
     )(counts, split, queries, fresh, own, other, gathered, cosine, sine)
@@ -379,14 +395,24 @@
 ):
     holders = lax.axis_size(POOL)
     capacity = holder_list.shape[1] // holders
-    outgoing = pack_blocks(tail_counts, holder_list, slot_list, kv_store[:, :, 0, :], capacity // 2)
-    own = lax.all_to_all(outgoing, POOL, split_axis=0, concat_axis=0, tiled=True)
-    counts, arrived = head_sums(
-        tail_counts, holder_list, head_hidden[0], norm_gain[None, :], kv_weight, lax.axis_size("y"), holders
+    packed, send, keep, counts = prepare(
+        tail_counts,
+        holder_list,
+        slot_list,
+        head_hidden[0],
+        norm_gain,
+        kv_weight,
+        kv_store[:, :, 0, :],
+        capacity // 2,
+        holders,
+        lax.axis_size("y"),
     )
-    own, arrived = lax.optimization_barrier((own, arrived))
+    own = lax.all_to_all(packed, POOL, split_axis=0, concat_axis=0, tiled=True)
+    turns = join_cores(lax.all_gather(send, "core", axis=0), keep)
+    arrived = [lax.ppermute(turn, COMP, owners_of_turn(t)) for t, turn in enumerate(turns)]
+    gathered = lax.all_gather(join_chips(arrived), QUAD, axis=0)
+    own, gathered = lax.optimization_barrier((own, gathered))
     other = lax.ppermute(own, "core", SWAP)
-    gathered = lax.all_gather(join_chips(arrived), QUAD, axis=0)
     return attend(
         counts,
         split_blocks,

time: 82.2 us -> 69.3 us (0.84); the launches traced: 80.9 us -> 68.8 us
  Pallas kernels: 27 us -> 21.4 us
  waiting for transfers between devices: 7.13 us -> 4 us
  local copies, waits for them, and re-layouts: 2.38 us -> 0.04 us
  blocking collectives: 7.02 us -> 8.5 us
  starting transfers between devices: 35.3 us -> 33.9 us
  other arithmetic: 1.08 us -> 0 us
    ppermute x5 -> x4, waiting for transfers between devices: 7.13 us -> 2.38 us  [per_device(): lax.ppermute(turn, COMP, owners_of_turn(t))]
    pallas_call x3 -> x2, Pallas kernels: 9.02 us -> 5.45 us  [the longest x1 5.37 us: prepare(): pl.pallas_call(prepare_kernel, out_shape=(jax.ShapeDtypeStruct(packed, BF...]
    all_gather x0 -> x1, blocking collectives: none -> 2.62 us  [per_device(): turns = join_cores(lax.all_gather(send, 'core', axis=0), keep)]
    ppermute x5 -> x4, starting transfers between devices: 19.5 us -> 17.3 us  [per_device(): lax.ppermute(turn, COMP, owners_of_turn(t))]
    unnamed x16 -> x14, local copies, waits for them, and re-layouts: 1.81 us -> 0.04 us
    pallas_call x1, Pallas kernels: 1.66 us -> 0.04 us  [join_chips(): pl.pallas_call(join_chips_kernel, out_shape=jax.ShapeDtypeStruct(arrived[...]
    ppermute x1, waiting for transfers between devices: 0.01 us -> 1.62 us  [per_device(): other = lax.ppermute(own, 'core', SWAP)]
    all_gather x1, blocking collectives: 7.02 us -> 5.88 us  [per_device(): gathered = lax.all_gather(join_chips(arrived), QUAD, axis=0)]
  transfers between devices with their start and end apart: 7 -> 6, of which waited for: 3 -> 2; matrix products, arithmetic and copies ran while one was open for 2% -> 0% of each run, Pallas kernels for 8% -> 0%
where the time goes in v3:
time: 69.3 us; the launch traced here: 68.8 us
  starting transfers between devices  33.9 us (49%)
  Pallas kernels  21.4 us (31%)
  blocking collectives  8.5 us (12%)
  waiting for transfers between devices  4 us (6%)
  between operations  0.97 us (1%)
    ppermute x4, starting transfers between devices, per_device(): lax.ppermute(turn, COMP, owners_of_turn(t))  17.3 us
    pallas_call x1, Pallas kernels, attend(): pl.pallas_call(functools.partial(attend_kernel, min(512, rows), 512, widt...  15.9 us
    all_to_all x1, starting transfers between devices, per_device(): own = lax.all_to_all(packed, POOL, split_axis=0, concat_axis=0, tiled=True)  13.5 us
    all_gather x1, blocking collectives, per_device(): gathered = lax.all_gather(join_chips(arrived), QUAD, axis=0)  5.88 us
    pallas_call x1, Pallas kernels, prepare(): pl.pallas_call(prepare_kernel, out_shape=(jax.ShapeDtypeStruct(packed, BF...  5.37 us
    ppermute x1, starting transfers between devices, per_device(): other = lax.ppermute(own, 'core', SWAP)  3.12 us
    all_gather x1, blocking collectives, per_device(): turns = join_cores(lax.all_gather(send, 'core', axis=0), keep)  2.62 us
    ppermute x4, waiting for transfers between devices, per_device(): lax.ppermute(turn, COMP, owners_of_turn(t))  2.38 us
  transfers between devices with their start and end apart: 6, of which 2 were waited for; matrix products, arithmetic and copies ran while one was open for 0% of the time, Pallas kernels for 0%

profile of v3, /device:TPU:1, one launch (start us, length us, event | category | flops | bytes accessed | tf_op | source)
XLA Modules:
  0.0 68.8 jit_solution(238621177645107773)
XLA Ops:
  0.0 5.4 %prepare.1 = (bf16[16,128,256]{2,1,0:T(8,128)(2,1)}, bf16[4,144,256]{2,1,0:T(8,128)(2,1)}, f32[4,144,256]{2,1,0:T(8,128)}, s32[16,128]{1,0:T(8,128)}) custom-call(s32[16]{0:T(128)} %tail_ref.1, s32[16,64]{1,0:T(8,128)} %holder_ref.1, s32[16,64]{1,0:T(8,128)} %slot_ref.1, bf16[128,256]{1,0:T(8,128)(2,1)} %bitcast.12, bf16[256]{0:T(256)(128)(2,1)} %gain_ref.1, ...), custom_call_target="tpu_custom_call" | custom-call | tf_op jit(solution)/shard_map/prepare/pallas_call | solution.py:162
  5.4 0.0 copy-start.6
  5.4 0.0 copy-start
  5.4 0.0 copy-start.1
  5.4 0.0 copy-start.2
  5.4 0.0 copy-start.3
  5.4 0.0 copy-start.4
  5.4 0.0 copy-start.5
  5.5 13.5 %all-to-all-start = ((bf16[16,128,256]{2,1,0:T(8,128)(2,1)}), bf16[16,128,256]{2,1,0:T(8,128)(2,1)S(1)}, u32[]{:S(2)}, u32[]{:S(2)}) async-start(bf16[16,128,256]{2,1,0:T(8,128)(2,1)} %get-tuple-element.16), calls=%async_computation | async-start | bytes 2097152 | tf_op jit(solution)/shard_map/all_to_all | solution.py:410
  19.0 0.0 copy-done.6
  19.0 2.6 %all-gather = bf16[8,144,256]{2,1,0:T(8,128)(2,1)S(1)} all-gather(bf16[4,144,256]{2,1,0:T(8,128)(2,1)S(1)} %copy-done.6), channel_id=2, replica_groups=mesh['xh'=2,'z'=8,'y'=8,'xl'=2,'core'=2] {'core'}, dimensions={0}, use_global_device_ids=true | all-gather | bytes 884736 | tf_op jit(solution)/shard_map/all_gather | solution.py:411
  21.6 0.0 copy-done
  21.6 0.1 join_cores.1
  21.7 7.5 %collective-permute-start = (bf16[144,256]{1,0:T(8,128)(2,1)S(1)}, bf16[144,256]{1,0:T(8,128)(2,1)S(1)}, u32[]{:S(2)}, u32[]{:S(2)}) collective-permute-start(bf16[144,256]{1,0:T(8,128)(2,1)S(1)} %get-tuple-element.19), channel_id=1, source_target_pairs={{0,12},{1,17},{2,14},{3,19},{4,16},{5,21},{6,18},{7,23},{8,20},{9,... | collective-permute-start | bytes 221192 | tf_op jit(solution)/shard_map/ppermute | solution.py:412
  29.1 1.9 %collective-permute-start.1 = (bf16[144,256]{1,0:T(8,128)(2,1)S(1)}, bf16[144,256]{1,0:T(8,128)(2,1)S(1)}, u32[]{:S(2)}, u32[]{:S(2)}) collective-permute-start(bf16[144,256]{1,0:T(8,128)(2,1)S(1)} %get-tuple-element.20), channel_id=1, source_target_pairs={{0,8},{1,21},{2,10},{3,23},{4,12},{5,25},{6,14},{7,27},{8,16},{9,2... | collective-permute-start | bytes 221192 | tf_op jit(solution)/shard_map/ppermute | solution.py:412
  31.0 4.9 %collective-permute-start.2 = (bf16[144,256]{1,0:T(8,128)(2,1)S(1)}, bf16[144,256]{1,0:T(8,128)(2,1)S(1)}, u32[]{:S(2)}, u32[]{:S(2)}) collective-permute-start(bf16[144,256]{1,0:T(8,128)(2,1)S(1)} %get-tuple-element.21), channel_id=1, source_target_pairs={{0,4},{1,25},{2,6},{3,27},{4,8},{5,29},{6,10},{7,31},{8,12},{9,1},... | collective-permute-start | bytes 221192 | tf_op jit(solution)/shard_map/ppermute | solution.py:412
  36.0 3.0 %collective-permute-start.3 = (bf16[144,256]{1,0:T(8,128)(2,1)S(1)}, bf16[144,256]{1,0:T(8,128)(2,1)S(1)}, u32[]{:S(2)}, u32[]{:S(2)}) collective-permute-start(bf16[144,256]{1,0:T(8,128)(2,1)S(1)} %get-tuple-element.22), channel_id=1, source_target_pairs={{0,0},{1,29},{2,2},{3,31},{4,4},{5,1},{6,6},{7,3},{8,8},{9,5},{10,... | collective-permute-start | bytes 221192 | tf_op jit(solution)/shard_map/ppermute | solution.py:412
  39.0 0.0 collective-permute-done.refs_0_
  39.0 0.0 collective-permute-done.1.refs_1_
  39.0 0.0 collective-permute-done.2.refs_2_
  39.0 2.4 %collective-permute-done.3.refs_3_ = bf16[144,256]{1,0:T(8,128)(2,1)S(1)} collective-permute-done((bf16[144,256]{1,0:T(8,128)(2,1)S(1)}, bf16[144,256]{1,0:T(8,128)(2,1)S(1)}, u32[]{:S(2)}, u32[]{:S(2)}) %collective-permute-start.3) | collective-permute-done | bytes 73760 | tf_op jit(solution)/shard_map/ppermute | solution.py:412
  41.4 5.9 %all-gather.1 = bf16[576,256]{1,0:T(8,128)(2,1)S(1)} all-gather(bf16[144,256]{1,0:T(8,128)(2,1)S(1)} %join_chips.1), channel_id=3, replica_groups=mesh['xh'=2,'z'=8,'y'=8,'xl'=2,'core'=2] {'xl','core'}, dimensions={0}, use_global_device_ids=true | all-gather | bytes 368640 | tf_op jit(solution)/shard_map/all_gather | solution.py:413
  47.3 0.0 all-to-all-done.own_ref
  47.3 3.1 %collective-permute-start.4 = (bf16[16,128,256]{2,1,0:T(8,128)(2,1)S(1)}, bf16[16,128,256]{2,1,0:T(8,128)(2,1)S(1)}, u32[]{:S(2)}, u32[]{:S(2)}) collective-permute-start(bf16[16,128,256]{2,1,0:T(8,128)(2,1)S(1)} %all-to-all-done.own_ref), channel_id=1, source_target_pairs={{0,1},{1,0},{2,3},{3,2},{4,5},{5,4},{6,7},{7,6},{8,9},{9,8},{10,11... | collective-permute-start | bytes 3145736 | tf_op jit(solution)/shard_map/ppermute | solution.py:415
  51.1 1.6 %collective-permute-done.4.other_ref = bf16[16,128,256]{2,1,0:T(8,128)(2,1)S(1)} collective-permute-done((bf16[16,128,256]{2,1,0:T(8,128)(2,1)S(1)}, bf16[16,128,256]{2,1,0:T(8,128)(2,1)S(1)}, u32[]{:S(2)}, u32[]{:S(2)}) %collective-permute-start.4) | collective-permute-done | bytes 1048608 | tf_op jit(solution)/shard_map/ppermute | solution.py:415
  52.7 0.0 copy-done.1
  52.7 0.0 copy-done.2
  52.7 0.0 copy-done.3
  52.7 0.0 copy-done.4
  52.7 0.0 copy-done.5
  52.7 15.9 %attend.1 = bf16[1024,256]{1,0:T(8,128)(2,1)} custom-call(s32[16,128]{1,0:T(8,128)S(1)} %copy-done.3, s32[1]{0:T(128)S(6)} %copy.13.split_ref, bf16[1024,256]{1,0:T(8,128)(2,1)S(1)} %bitcast.9, bf16[1024,256]{1,0:T(8,128)(2,1)S(1)} %bitcast.10, bf16[16,128,256]{2,1,0:T(8,128)(2,1)S(1)} %all-to-all-done.own_ref, ...), custom_call_target="tpu_custom_call" | custom-call | flops 17179869184 | bytes 4194304 | tf_op jit(solution)/shard_map/attend/pallas_call | solution.py:368
  (1 shorter events, 0.0 us)
Async XLA Ops:
  5.4 13.6 %copy-start.6 = (bf16[4,144,256]{2,1,0:T(8,128)(2,1)S(1)}, bf16[4,144,256]{2,1,0:T(8,128)(2,1)}, u32[]{:S(2)}) copy-start(bf16[4,144,256]{2,1,0:T(8,128)(2,1)} %get-tuple-element.17) | copy-start | bytes 884740
  5.4 16.2 %copy-start = (f32[4,144,256]{2,1,0:T(8,128)S(1)}, f32[4,144,256]{2,1,0:T(8,128)}, u32[]{:S(2)}) copy-start(f32[4,144,256]{2,1,0:T(8,128)} %get-tuple-element.18.mine_ref) | copy-start | bytes 1769476
  5.4 47.3 %copy-start.1 = (bf16[1,1024,256]{2,1,0:T(8,128)(2,1)S(1)}, bf16[1,1024,256]{2,1,0:T(8,128)(2,1)}, u32[]{:S(2)}) copy-start(bf16[1,1024,256]{2,1,0:T(8,128)(2,1)} %param.12) | copy-start | bytes 1572868
  5.4 47.3 %copy-start.2 = (bf16[1,1024,1,256]{3,1,2,0:T(8,128)(2,1)S(1)}, bf16[1,1024,1,256]{3,1,2,0:T(8,128)(2,1)}, u32[]{:S(2)}) copy-start(bf16[1,1024,1,256]{3,1,2,0:T(8,128)(2,1)} %param.13) | copy-start | bytes 1572868
  5.4 47.3 %copy-start.3 = (s32[16,128]{1,0:T(8,128)S(1)}, s32[16,128]{1,0:T(8,128)}, u32[]{:S(2)}) copy-start(s32[16,128]{1,0:T(8,128)} %get-tuple-element.15.counts_ref) | copy-start | bytes 24580
  5.4 47.3 %copy-start.4 = (f32[128,128]{1,0:T(8,128)S(1)}, f32[128,128]{1,0:T(8,128)}, u32[]{:S(2)}) copy-start(f32[128,128]{1,0:T(8,128)} %constant.4.clone.cos_ref) | copy-start | bytes 196612
  5.4 47.3 %copy-start.5 = (f32[128,128]{1,0:T(8,128)S(1)}, f32[128,128]{1,0:T(8,128)}, u32[]{:S(2)}) copy-start(f32[128,128]{1,0:T(8,128)} %constant.5.clone.sin_ref) | copy-start | bytes 196612
  5.5 41.8 %all-to-all-start = ((bf16[16,128,256]{2,1,0:T(8,128)(2,1)}), bf16[16,128,256]{2,1,0:T(8,128)(2,1)S(1)}, u32[]{:S(2)}, u32[]{:S(2)}) async-start(bf16[16,128,256]{2,1,0:T(8,128)(2,1)} %get-tuple-element.16), calls=%async_computation | async-start | bytes 2097152 | tf_op jit(solution)/shard_map/all_to_all | solution.py:410
  21.7 17.3 %collective-permute-start = (bf16[144,256]{1,0:T(8,128)(2,1)S(1)}, bf16[144,256]{1,0:T(8,128)(2,1)S(1)}, u32[]{:S(2)}, u32[]{:S(2)}) collective-permute-start(bf16[144,256]{1,0:T(8,128)(2,1)S(1)} %get-tuple-element.19), channel_id=1, source_target_pairs={{0,12},{1,17},{2,14},{3,19},{4,16},{5,21},{6,18},{7,23},{8,20},{9,... | collective-permute-start | bytes 221192 | tf_op jit(solution)/shard_map/ppermute | solution.py:412
  29.1 9.8 %collective-permute-start.1 = (bf16[144,256]{1,0:T(8,128)(2,1)S(1)}, bf16[144,256]{1,0:T(8,128)(2,1)S(1)}, u32[]{:S(2)}, u32[]{:S(2)}) collective-permute-start(bf16[144,256]{1,0:T(8,128)(2,1)S(1)} %get-tuple-element.20), channel_id=1, source_target_pairs={{0,8},{1,21},{2,10},{3,23},{4,12},{5,25},{6,14},{7,27},{8,16},{9,2... | collective-permute-start | bytes 221192 | tf_op jit(solution)/shard_map/ppermute | solution.py:412
  31.0 7.9 %collective-permute-start.2 = (bf16[144,256]{1,0:T(8,128)(2,1)S(1)}, bf16[144,256]{1,0:T(8,128)(2,1)S(1)}, u32[]{:S(2)}, u32[]{:S(2)}) collective-permute-start(bf16[144,256]{1,0:T(8,128)(2,1)S(1)} %get-tuple-element.21), channel_id=1, source_target_pairs={{0,4},{1,25},{2,6},{3,27},{4,8},{5,29},{6,10},{7,31},{8,12},{9,1},... | collective-permute-start | bytes 221192 | tf_op jit(solution)/shard_map/ppermute | solution.py:412
  36.0 5.4 %collective-permute-start.3 = (bf16[144,256]{1,0:T(8,128)(2,1)S(1)}, bf16[144,256]{1,0:T(8,128)(2,1)S(1)}, u32[]{:S(2)}, u32[]{:S(2)}) collective-permute-start(bf16[144,256]{1,0:T(8,128)(2,1)S(1)} %get-tuple-element.22), channel_id=1, source_target_pairs={{0,0},{1,29},{2,2},{3,31},{4,4},{5,1},{6,6},{7,3},{8,8},{9,5},{10,... | collective-permute-start | bytes 221192 | tf_op jit(solution)/shard_map/ppermute | solution.py:412
  47.3 5.4 %collective-permute-start.4 = (bf16[16,128,256]{2,1,0:T(8,128)(2,1)S(1)}, bf16[16,128,256]{2,1,0:T(8,128)(2,1)S(1)}, u32[]{:S(2)}, u32[]{:S(2)}) collective-permute-start(bf16[16,128,256]{2,1,0:T(8,128)(2,1)S(1)} %all-to-all-done.own_ref), channel_id=1, source_target_pairs={{0,1},{1,0},{2,3},{3,2},{4,5},{5,4},{6,7},{7,6},{8,9},{9,8},{10,11... | collective-permute-start | bytes 3145736 | tf_op jit(solution)/shard_map/ppermute | solution.py:415

commit v4 on v3

--- a/solution.py
+++ b/solution.py
@@ -48,12 +48,9 @@
     cell = lax.broadcasted_iota(jnp.int32, (holders, cells), 1)
     match = (holder_ref[pl.ds(session, 1), :] == holder) & (cell < tail_ref[session])
     found = jnp.sum(jnp.where(match, 1.0, 0.0), axis=1, keepdims=True).astype(jnp.int32)
-    ids = lax.broadcasted_iota(jnp.int32, (holders, 1), 0)
-    full = jnp.max(jnp.where(found >= cells // holders, ids, 0).astype(F32), axis=0, keepdims=True)
     lane = lax.broadcasted_iota(jnp.int32, counts_ref.shape, 1)
     counts = jnp.where(lane == 0, found, 0)
-    counts = jnp.where(lane == 1, full.astype(jnp.int32), counts)
-    counts_ref[...] = jnp.where(lane == 2, lax.axis_index("core"), counts)
+    counts_ref[...] = jnp.where(lane == 1, lax.axis_index("core"), counts)
 
 
 def offsets(turn):
@@ -88,20 +85,17 @@
 
 def prepare_kernel(tail_ref, holder_ref, slot_ref, hidden_ref, gain_ref, weight_hbm, store_ref,
                    packed_ref, send_ref, keep_ref, counts_ref,
-                   index_vmem, index_smem, staged, weight_ref, send, keep, sems, in_sems, out_sems):
+                   counts, staged, weight_ref, send, keep, sems, in_sems, out_sems):
     sessions = holder_ref.shape[0]
     block_rows = store_ref.shape[1]
     share = packed_ref.shape[1] // block_rows
     weight_copy = pltpu.make_async_copy(weight_hbm, weight_ref, sems.at[0])
     weight_copy.start()
-    index_vmem[...] = held_slots(share, tail_ref, holder_ref, slot_ref)
-    index_copy = pltpu.make_async_copy(index_vmem, index_smem, sems.at[1])
-    index_copy.start()
-    index_copy.wait()
+    slots = held_slots(share, tail_ref, holder_ref, slot_ref)
 
     def block_in(s, k):
         return pltpu.make_async_copy(
-            store_ref.at[index_smem[s, k]],
+            store_ref.at[slots[s, k]],
             staged.at[s, pl.ds(k * block_rows, block_rows)],
             in_sems.at[s * share + k],
         )
@@ -141,7 +135,9 @@
         keep[t, rows:, :] = jnp.concatenate([squares, jnp.zeros_like(squares)], axis=1)
     keep_copy = pltpu.make_async_copy(keep, keep_ref, sems.at[3])
     keep_copy.start()
-    block_counts(tail_ref, holder_ref, counts_ref)
+    block_counts(tail_ref, holder_ref, counts)
+    counts_copy = pltpu.make_async_copy(counts, counts_ref, sems.at[1])
+    counts_copy.start()
 
     for s in range(sessions):
         for k in range(share):
@@ -149,6 +145,7 @@
         slab_out(s).start()
     send_copy.wait()
     keep_copy.wait()
+    counts_copy.wait()
     for s in range(sessions):
         slab_out(s).wait()
 
@@ -168,10 +165,9 @@
             jax.ShapeDtypeStruct((holders, 128), jnp.int32),
         ),
         in_specs=[SMEM, VMEM, VMEM, VMEM, VMEM, anywhere, anywhere],
-        out_specs=(anywhere, anywhere, anywhere, VMEM),
+        out_specs=(anywhere,) * 4,
         scratch_shapes=[
-            pltpu.VMEM((sessions, 128), jnp.int32),
-            pltpu.SMEM((sessions, 128), jnp.int32),
+            pltpu.VMEM((holders, 128), jnp.int32),
             pltpu.VMEM(packed, BF16),
             pltpu.VMEM(weight.shape, BF16),
             pltpu.VMEM(partials, BF16),
@@ -270,16 +266,62 @@
     return peak, mixed
 
 
-def attend_kernel(block, chunk, width_total, counts_ref, split_ref, queries_ref, fresh_ref, own_ref, other_ref,
-                  gathered_ref, cos_ref, sin_ref, out_ref, blocks, live, sems):
+def doubled(keys):
+    return jnp.concatenate([keys, keys], axis=1)
+
+
+def block_queries(queries_ref, here, head_dim):
+    return [
+        scaled_queries(queries_ref[here, start : start + head_dim], head_dim)
+        for start in range(0, queries_ref.shape[1], head_dim)
+    ]
+
+
+def fresh_kernel(block, queries_ref, fresh_ref, peak_ref, mixed_ref):
+    head_dim = fresh_ref.shape[1] // 2
+    row = lax.broadcasted_iota(jnp.int32, (block, block), 0)
+    column = lax.broadcasted_iota(jnp.int32, (block, block), 1)
+    for b in range(queries_ref.shape[0] // block):
+        here = pl.ds(b * block, block)
+        query = block_queries(queries_ref, here, head_dim)
+        state = [None] * len(query)
+        for earlier in range(b + 1):
+            there = pl.ds(earlier * block, block)
+            keys = doubled(fresh_ref[there, :head_dim])
+            values = fresh_ref[there, head_dim:]
+            values = jnp.concatenate([values, jnp.ones_like(values)], axis=1)
+            for h in range(len(query)):
+                state[h] = extend(state[h], query[h], keys, values, column <= row if earlier == b else None)
+        for h, (peak, mixed) in enumerate(state):
+            peak_ref[h, here, :] = jnp.broadcast_to(peak, (block, 128))
+            mixed_ref[h, here, :] = mixed
+
+
+def attend_fresh(queries, fresh):
+    rows, width = queries.shape
+    heads = 2 * width // fresh.shape[1]
+    return pl.pallas_call(
+        functools.partial(fresh_kernel, min(512, rows)),
+        in_specs=[VMEM, VMEM],
+        out_specs=(VMEM, VMEM),
+        out_shape=(
+            jax.ShapeDtypeStruct((heads, rows, 128), F32),
+            jax.ShapeDtypeStruct((heads, rows, fresh.shape[1]), F32),
+        ),
+        compiler_params=params(24),
+        cost_estimate=pl.CostEstimate(flops=2**31, bytes_accessed=2**21, transcendentals=2**20),
+        name="attend_fresh",
+    )(queries, fresh)
+
+
+def attend_kernel(block, chunk, width_total, counts_ref, split_ref, queries_ref, fresh_ref, peak_ref, mixed_ref,
+                  own_ref, other_ref, gathered_ref, cos_ref, sin_ref, out_ref, blocks, live, sems):
     holders, slab, width = own_ref.shape
     head_dim = width // 2
     head_rows = gathered_ref.shape[1] - EXTRA
-    loaded_rows = 2 * holders * slab
     share = 2
     rows = slab // share
-    full = counts_ref[0, 1]
-    core = counts_ref[0, 2]
+    core = counts_ref[0, 1]
     copies = [
         pltpu.make_async_copy(ref, blocks.at[pl.ds(side * holders, holders)], sems.at[side])
         for side, ref in enumerate((own_ref, other_ref))
@@ -287,98 +329,79 @@
     for copy in copies:
         copy.start()
     live[...] = jnp.ones(live.shape, BF16)
-
-    def gather_blocks():
-        for copy in copies:
-            copy.wait()
-
-        def mend(holder, _):
-            for side in range(2):
-                for k in range(share):
-
-                    @pl.when((core if side == 0 else 1 - core) * share + k >= counts_ref[holder, 0])
-                    def _():
-                        here = pl.ds(k * rows, rows)
-                        place = side * holders + holder
-                        spare = side * holders + full
-                        blocks[place, here, :head_dim] = blocks[spare, here, :head_dim]
-                        blocks[place, here, head_dim:] = jnp.zeros((rows, head_dim), BF16)
-                        live[place, here, :] = jnp.zeros((rows, head_dim), BF16)
+    spare = fresh_ref[:16, :head_dim].astype(F32)[:1]
+
+    position = lax.broadcasted_iota(jnp.int32, (head_rows, head_dim), 0)
+    admitted = position < jnp.reshape(split_ref[...], (1, 1)) * rows
+    keys, values = finish_head(width_total, gathered_ref, cos_ref, sin_ref)
+    head_keys = jnp.where(admitted, keys, spare).astype(BF16)
+    head_values = jnp.where(admitted, values, 0.0).astype(BF16)
+    head_live = jnp.where(admitted, 1.0, 0.0).astype(BF16)
+
+    def mend(side):
+        copies[side].wait()
+
+        def mend_holder(holder, _):
+            for k in range(share):
+
+                @pl.when((core if side == 0 else 1 - core) * share + k >= counts_ref[holder, 0])
+                def _():
+                    here = pl.ds(k * rows, rows)
+                    place = side * holders + holder
+                    blocks[place, here, :head_dim] = jnp.broadcast_to(spare, (rows, head_dim)).astype(BF16)
+                    blocks[place, here, head_dim:] = jnp.zeros((rows, head_dim), BF16)
+                    live[place, here, :] = jnp.zeros((rows, head_dim), BF16)
 
             return 0
 
-        lax.fori_loop(0, holders, mend, 0)
-        position = lax.broadcasted_iota(jnp.int32, (head_rows, head_dim), 0)
-        admitted = position < split_ref[0] * rows
-        keys, values = finish_head(width_total, gathered_ref, cos_ref, sin_ref)
-        spare = blocks[full, :16, :head_dim].astype(F32)[:1]
-        blocks[2 * holders, :head_rows, :head_dim] = jnp.where(admitted, keys, spare).astype(BF16)
-        blocks[2 * holders, :head_rows, head_dim:] = jnp.where(admitted, values, 0.0).astype(BF16)
-        live[2 * holders, :head_rows, :] = jnp.where(admitted, 1.0, 0.0).astype(BF16)
-
-    heads = queries_ref.shape[1] // head_dim
-    total_rows = queries_ref.shape[0]
-    row = lax.broadcasted_iota(jnp.int32, (block, block), 0)
-    column = lax.broadcasted_iota(jnp.int32, (block, block), 1)
+        lax.fori_loop(0, holders, mend_holder, 0)
+
     step = chunk // slab
-    starts = list(range(0, 2 * holders, step))
-
-    def doubled(keys):
-        return jnp.concatenate([keys, keys], axis=1)
-
-    for b in range(total_rows // block):
+    for b in range(queries_ref.shape[0] // block):
         here = pl.ds(b * block, block)
-        query = [
-            scaled_queries(queries_ref[here, h * head_dim : (h + 1) * head_dim], head_dim) for h in range(heads)
+        query = block_queries(queries_ref, here, head_dim)
+        state = [
+            (jnp.max(peak_ref[h, here, :], axis=1, keepdims=True), mixed_ref[h, here, :])
+            for h in range(len(query))
         ]
-        state = [None] * heads
-        for earlier in range(b + 1):
-            there = pl.ds(earlier * block, block)
-            keys = doubled(fresh_ref[there, :head_dim])
-            values = fresh_ref[there, head_dim:]
-            values = jnp.concatenate([values, jnp.ones_like(values)], axis=1)
-            for h in range(heads):
-                mask = column <= row if earlier == b else None
-                state[h] = extend(state[h], query[h], keys, values, mask)
-        if b == 0:
-            gather_blocks()
-        for start in starts:
-            parts = list(range(start, start + step))
-            taken = [blocks[i] for i in parts]
-            weights = [live[i] for i in parts]
-            if start == starts[-1]:
-                taken.append(blocks[2 * holders, :head_rows])
-                weights.append(live[2 * holders, :head_rows])
-            taken = jnp.concatenate(taken, axis=0)
-            values = jnp.concatenate([taken[:, head_dim:], jnp.concatenate(weights, axis=0)], axis=1)
-            for h in range(heads):
-                state[h] = extend(state[h], query[h], doubled(taken[:, :head_dim]), values)
-        for h in range(heads):
-            mixed = state[h][1]
+        for start in range(0, 2 * holders, step):
+            if b == 0 and start % holders == 0:
+                mend(start // holders)
+            taken = jnp.concatenate([blocks[i] for i in range(start, start + step)], axis=0)
+            keys, values = taken[:, :head_dim], taken[:, head_dim:]
+            weights = jnp.concatenate([live[i] for i in range(start, start + step)], axis=0)
+            if start == 0:
+                keys = jnp.concatenate([head_keys, keys], axis=0)
+                values = jnp.concatenate([head_values, values], axis=0)
+                weights = jnp.concatenate([head_live, weights], axis=0)
+            values = jnp.concatenate([values, weights], axis=1)
+            for h in range(len(query)):
+                state[h] = extend(state[h], query[h], doubled(keys), values)
+        for h, (_, mixed) in enumerate(state):
             out_ref[here, h * head_dim : (h + 1) * head_dim] = (
                 mixed[:, :head_dim] / mixed[:, head_dim:]
             ).astype(BF16)
 
 
-def attend(counts, split, queries, fresh, own, other, gathered, width_total):
+def attend(counts, split, queries, fresh, peak, mixed, own, other, gathered, width_total):
     rows, width = queries.shape
     holders, slab, pair = own.shape
     cosine, sine = rotation(gathered.shape[1] - EXTRA, pair // 2)
     anywhere = pl.BlockSpec(memory_space=pl.ANY)
     return pl.pallas_call(
         functools.partial(attend_kernel, min(512, rows), 512, width_total),
-        in_specs=[SMEM, SMEM, VMEM, VMEM, anywhere, anywhere, VMEM, VMEM, VMEM],
+        in_specs=[SMEM, VMEM, VMEM, VMEM, VMEM, VMEM, anywhere, anywhere, VMEM, VMEM, VMEM],
         out_specs=VMEM,
         scratch_shapes=[
-            pltpu.VMEM((2 * holders + 1, slab, pair), BF16),
-            pltpu.VMEM((2 * holders + 1, slab, pair // 2), BF16),
+            pltpu.VMEM((2 * holders, slab, pair), BF16),
+            pltpu.VMEM((2 * holders, slab, pair // 2), BF16),
             pltpu.SemaphoreType.DMA((2,)),
         ],
         out_shape=jax.ShapeDtypeStruct((rows, width), BF16),
         compiler_params=params(24),
         cost_estimate=pl.CostEstimate(flops=2**34, bytes_accessed=2**22, transcendentals=2**23),
         name="attend",
-    )(counts, split, queries, fresh, own, other, gathered, cosine, sine)
+    )(counts, split, queries, fresh, peak, mixed, own, other, gathered, cosine, sine)
 
 
 def per_device(
@@ -411,13 +434,17 @@
     turns = join_cores(lax.all_gather(send, "core", axis=0), keep)
     arrived = [lax.ppermute(turn, COMP, owners_of_turn(t)) for t, turn in enumerate(turns)]
     gathered = lax.all_gather(join_chips(arrived), QUAD, axis=0)
-    own, gathered = lax.optimization_barrier((own, gathered))
+    own, gathered, queries = lax.optimization_barrier((own, gathered, queries))
     other = lax.ppermute(own, "core", SWAP)
+    fresh = fresh_kv[0, :, 0, :]
+    peak, mixed = attend_fresh(queries[0], fresh)
     return attend(
         counts,
         split_blocks,
         queries[0],
-        fresh_kv[0, :, 0, :],
+        fresh,
+        peak,
+        mixed,
         own,
         other,
         gathered,

time: 69.3 us -> 67.5 us (0.974)
  waiting for transfers between devices: 4 us -> 2.39 us
    pallas_call x0 -> x1, Pallas kernels: none -> 2.19 us  [attend_fresh(): pl.pallas_call(functools.partial(fresh_kernel, min(512, rows)), in_specs=...]
    ppermute x1, waiting for transfers between devices: 1.62 us -> 0.01 us  [per_device(): other = lax.ppermute(own, 'core', SWAP)]
    pallas_call x1, Pallas kernels: 15.9 us -> 14.6 us  [attend(): pl.pallas_call(functools.partial(attend_kernel, min(512, rows), 512, widt...]
    pallas_call x1, Pallas kernels: 5.37 us -> 4.3 us  [prepare(): pl.pallas_call(prepare_kernel, out_shape=(jax.ShapeDtypeStruct(packed, BF...]
  transfers between devices with their start and end apart: 6 -> 6, of which waited for: 2 -> 1; matrix products, arithmetic and copies ran while one was open for 0% -> 0% of each run, Pallas kernels for 0% -> 3%
where the time goes in v4:
time: 67.5 us; the launch traced here: 67.1 us
  starting transfers between devices  33.9 us (50%)
  Pallas kernels  21.2 us (31%)
  blocking collectives  8.53 us (13%)
  waiting for transfers between devices  2.39 us (4%)
  between operations  1.01 us (1%)
    ppermute x4, starting transfers between devices, per_device(): lax.ppermute(turn, COMP, owners_of_turn(t))  17.3 us
    pallas_call x1, Pallas kernels, attend(): pl.pallas_call(functools.partial(attend_kernel, min(512, rows), 512, widt...  14.6 us
    all_to_all x1, starting transfers between devices, per_device(): own = lax.all_to_all(packed, POOL, split_axis=0, concat_axis=0, tiled=True)  13.6 us
    all_gather x1, blocking collectives, per_device(): gathered = lax.all_gather(join_chips(arrived), QUAD, axis=0)  5.88 us
    pallas_call x1, Pallas kernels, prepare(): pl.pallas_call(prepare_kernel, out_shape=(jax.ShapeDtypeStruct(packed, BF...  4.3 us
    ppermute x1, starting transfers between devices, per_device(): other = lax.ppermute(own, 'core', SWAP)  3.1 us
    all_gather x1, blocking collectives, per_device(): turns = join_cores(lax.all_gather(send, 'core', axis=0), keep)  2.65 us
    ppermute x4, waiting for transfers between devices, per_device(): lax.ppermute(turn, COMP, owners_of_turn(t))  2.38 us
  transfers between devices with their start and end apart: 6, of which 1 were waited for; matrix products, arithmetic and copies ran while one was open for 0% of the time, Pallas kernels for 3%

profile of v4, /device:TPU:1, one launch (start us, length us, event | category | flops | bytes accessed | tf_op | source)
XLA Modules:
  0.0 67.1 jit_solution(7828490990458746394)
XLA Ops:
  0.0 4.3 %prepare.1 = (bf16[16,128,256]{2,1,0:T(8,128)(2,1)}, bf16[4,144,256]{2,1,0:T(8,128)(2,1)}, f32[4,144,256]{2,1,0:T(8,128)}, s32[16,128]{1,0:T(8,128)}) custom-call(s32[16]{0:T(128)} %tail_ref.1, s32[16,64]{1,0:T(8,128)} %holder_ref.1, s32[16,64]{1,0:T(8,128)} %slot_ref.1, bf16[128,256]{1,0:T(8,128)(2,1)} %bitcast.14, bf16[256]{0:T(256)(128)(2,1)} %gain_ref.1, ...), custom_call_target="tpu_custom_call" | custom-call | tf_op jit(solution)/shard_map/prepare/pallas_call | solution.py:159
  4.3 0.0 copy-start.6
  4.3 0.0 copy-start
  4.3 0.0 copy-start.1
  4.3 0.0 copy-start.2
  4.4 13.6 %all-to-all-start = ((bf16[16,128,256]{2,1,0:T(8,128)(2,1)}), bf16[16,128,256]{2,1,0:T(8,128)(2,1)S(1)}, u32[]{:S(2)}, u32[]{:S(2)}) async-start(bf16[16,128,256]{2,1,0:T(8,128)(2,1)} %get-tuple-element.19), calls=%async_computation | async-start | bytes 2097152 | tf_op jit(solution)/shard_map/all_to_all | solution.py:433
  17.9 0.0 copy-done.6
  17.9 2.6 %all-gather = bf16[8,144,256]{2,1,0:T(8,128)(2,1)S(1)} all-gather(bf16[4,144,256]{2,1,0:T(8,128)(2,1)S(1)} %copy-done.6), channel_id=2, replica_groups=mesh['xh'=2,'z'=8,'y'=8,'xl'=2,'core'=2] {'core'}, dimensions={0}, use_global_device_ids=true | all-gather | bytes 884736 | tf_op jit(solution)/shard_map/all_gather | solution.py:434
  20.6 0.0 copy-done
  20.6 0.1 join_cores.1
  20.6 7.5 %collective-permute-start = (bf16[144,256]{1,0:T(8,128)(2,1)S(1)}, bf16[144,256]{1,0:T(8,128)(2,1)S(1)}, u32[]{:S(2)}, u32[]{:S(2)}) collective-permute-start(bf16[144,256]{1,0:T(8,128)(2,1)S(1)} %get-tuple-element.22), channel_id=1, source_target_pairs={{0,12},{1,17},{2,14},{3,19},{4,16},{5,21},{6,18},{7,23},{8,20},{9,... | collective-permute-start | bytes 221192 | tf_op jit(solution)/shard_map/ppermute | solution.py:435
  28.1 1.9 %collective-permute-start.1 = (bf16[144,256]{1,0:T(8,128)(2,1)S(1)}, bf16[144,256]{1,0:T(8,128)(2,1)S(1)}, u32[]{:S(2)}, u32[]{:S(2)}) collective-permute-start(bf16[144,256]{1,0:T(8,128)(2,1)S(1)} %get-tuple-element.23), channel_id=1, source_target_pairs={{0,8},{1,21},{2,10},{3,23},{4,12},{5,25},{6,14},{7,27},{8,16},{9,2... | collective-permute-start | bytes 221192 | tf_op jit(solution)/shard_map/ppermute | solution.py:435
  30.0 4.9 %collective-permute-start.2 = (bf16[144,256]{1,0:T(8,128)(2,1)S(1)}, bf16[144,256]{1,0:T(8,128)(2,1)S(1)}, u32[]{:S(2)}, u32[]{:S(2)}) collective-permute-start(bf16[144,256]{1,0:T(8,128)(2,1)S(1)} %get-tuple-element.24), channel_id=1, source_target_pairs={{0,4},{1,25},{2,6},{3,27},{4,8},{5,29},{6,10},{7,31},{8,12},{9,1},... | collective-permute-start | bytes 221192 | tf_op jit(solution)/shard_map/ppermute | solution.py:435
  35.0 3.0 %collective-permute-start.3 = (bf16[144,256]{1,0:T(8,128)(2,1)S(1)}, bf16[144,256]{1,0:T(8,128)(2,1)S(1)}, u32[]{:S(2)}, u32[]{:S(2)}) collective-permute-start(bf16[144,256]{1,0:T(8,128)(2,1)S(1)} %get-tuple-element.25), channel_id=1, source_target_pairs={{0,0},{1,29},{2,2},{3,31},{4,4},{5,1},{6,6},{7,3},{8,8},{9,5},{10,... | collective-permute-start | bytes 221192 | tf_op jit(solution)/shard_map/ppermute | solution.py:435
  37.9 0.0 collective-permute-done.refs_0_
  38.0 0.0 collective-permute-done.1.refs_1_
  38.0 0.0 collective-permute-done.2.refs_2_
  38.0 2.4 %collective-permute-done.3.refs_3_ = bf16[144,256]{1,0:T(8,128)(2,1)S(1)} collective-permute-done((bf16[144,256]{1,0:T(8,128)(2,1)S(1)}, bf16[144,256]{1,0:T(8,128)(2,1)S(1)}, u32[]{:S(2)}, u32[]{:S(2)}) %collective-permute-start.3) | collective-permute-done | bytes 73760 | tf_op jit(solution)/shard_map/ppermute | solution.py:435
  40.4 5.9 %all-gather.1 = bf16[576,256]{1,0:T(8,128)(2,1)S(1)} all-gather(bf16[144,256]{1,0:T(8,128)(2,1)S(1)} %join_chips.1), channel_id=3, replica_groups=mesh['xh'=2,'z'=8,'y'=8,'xl'=2,'core'=2] {'xl','core'}, dimensions={0}, use_global_device_ids=true | all-gather | bytes 368640 | tf_op jit(solution)/shard_map/all_gather | solution.py:436
  46.3 0.0 all-to-all-done.own_ref
  46.3 3.1 %collective-permute-start.4 = (bf16[16,128,256]{2,1,0:T(8,128)(2,1)S(1)}, bf16[16,128,256]{2,1,0:T(8,128)(2,1)S(1)}, u32[]{:S(2)}, u32[]{:S(2)}) collective-permute-start(bf16[16,128,256]{2,1,0:T(8,128)(2,1)S(1)} %all-to-all-done.own_ref), channel_id=1, source_target_pairs={{0,1},{1,0},{2,3},{3,2},{4,5},{5,4},{6,7},{7,6},{8,9},{9,8},{10,11... | collective-permute-start | bytes 3145736 | tf_op jit(solution)/shard_map/ppermute | solution.py:438
  50.0 0.0 copy-done.1
  50.0 0.0 copy-done.2
  50.1 0.0 copy-start.3
  50.1 0.0 copy-start.4
  50.1 0.0 copy-start.5
  50.1 2.2 %attend_fresh.1 = (f32[2,1024,128]{2,1,0:T(8,128)S(1)}, f32[2,1024,256]{2,1,0:T(8,128)S(1)}) custom-call(bf16[1024,256]{1,0:T(8,128)(2,1)S(1)} %bitcast.9, bf16[1024,256]{1,0:T(8,128)(2,1)S(1)} %bitcast.11), custom_call_target="tpu_custom_call" | custom-call | flops 2147483648 | bytes 2097152 | tf_op jit(solution)/shard_map/attend_fresh/pallas_call | solution.py:303
  52.3 0.0 collective-permute-done.4.other_ref
  52.3 0.0 copy-done.3
  52.3 0.0 copy-done.4
  52.3 0.0 copy-done.5
  52.3 14.6 %attend.1 = bf16[1024,256]{1,0:T(8,128)(2,1)} custom-call(s32[16,128]{1,0:T(8,128)S(1)} %copy-done.3, s32[1]{0:T(128)S(6)} %copy.13.split_ref, bf16[1024,256]{1,0:T(8,128)(2,1)S(1)} %bitcast.10, bf16[1024,256]{1,0:T(8,128)(2,1)S(1)} %bitcast.12, f32[2,1024,128]{2,1,0:T(8,128)S(1)} %get-tuple-element.27.peak_ref, ...), custom_call_target="tpu_custom_call" | custom-call | flops 17179869184 | bytes 4194304 | tf_op jit(solution)/shard_map/attend/pallas_call | solution.py:391
  (1 shorter events, 0.0 us)
Async XLA Ops:
  4.3 13.6 %copy-start.6 = (bf16[4,144,256]{2,1,0:T(8,128)(2,1)S(1)}, bf16[4,144,256]{2,1,0:T(8,128)(2,1)}, u32[]{:S(2)}) copy-start(bf16[4,144,256]{2,1,0:T(8,128)(2,1)} %get-tuple-element.20) | copy-start | bytes 884740
  4.3 16.3 %copy-start = (f32[4,144,256]{2,1,0:T(8,128)S(1)}, f32[4,144,256]{2,1,0:T(8,128)}, u32[]{:S(2)}) copy-start(f32[4,144,256]{2,1,0:T(8,128)} %get-tuple-element.21.mine_ref) | copy-start | bytes 1769476
  4.3 45.7 %copy-start.1 = (bf16[1,1024,256]{2,1,0:T(8,128)(2,1)S(1)}, bf16[1,1024,256]{2,1,0:T(8,128)(2,1)}, u32[]{:S(2)}) copy-start(bf16[1,1024,256]{2,1,0:T(8,128)(2,1)} %param.12) | copy-start | bytes 1572868
  4.3 45.7 %copy-start.2 = (bf16[1,1024,1,256]{3,1,2,0:T(8,128)(2,1)S(1)}, bf16[1,1024,1,256]{3,1,2,0:T(8,128)(2,1)}, u32[]{:S(2)}) copy-start(bf16[1,1024,1,256]{3,1,2,0:T(8,128)(2,1)} %param.13) | copy-start | bytes 1572868
  4.4 41.9 %all-to-all-start = ((bf16[16,128,256]{2,1,0:T(8,128)(2,1)}), bf16[16,128,256]{2,1,0:T(8,128)(2,1)S(1)}, u32[]{:S(2)}, u32[]{:S(2)}) async-start(bf16[16,128,256]{2,1,0:T(8,128)(2,1)} %get-tuple-element.19), calls=%async_computation | async-start | bytes 2097152 | tf_op jit(solution)/shard_map/all_to_all | solution.py:433
  20.6 17.3 %collective-permute-start = (bf16[144,256]{1,0:T(8,128)(2,1)S(1)}, bf16[144,256]{1,0:T(8,128)(2,1)S(1)}, u32[]{:S(2)}, u32[]{:S(2)}) collective-permute-start(bf16[144,256]{1,0:T(8,128)(2,1)S(1)} %get-tuple-element.22), channel_id=1, source_target_pairs={{0,12},{1,17},{2,14},{3,19},{4,16},{5,21},{6,18},{7,23},{8,20},{9,... | collective-permute-start | bytes 221192 | tf_op jit(solution)/shard_map/ppermute | solution.py:435
  28.1 9.8 %collective-permute-start.1 = (bf16[144,256]{1,0:T(8,128)(2,1)S(1)}, bf16[144,256]{1,0:T(8,128)(2,1)S(1)}, u32[]{:S(2)}, u32[]{:S(2)}) collective-permute-start(bf16[144,256]{1,0:T(8,128)(2,1)S(1)} %get-tuple-element.23), channel_id=1, source_target_pairs={{0,8},{1,21},{2,10},{3,23},{4,12},{5,25},{6,14},{7,27},{8,16},{9,2... | collective-permute-start | bytes 221192 | tf_op jit(solution)/shard_map/ppermute | solution.py:435
  30.0 7.9 %collective-permute-start.2 = (bf16[144,256]{1,0:T(8,128)(2,1)S(1)}, bf16[144,256]{1,0:T(8,128)(2,1)S(1)}, u32[]{:S(2)}, u32[]{:S(2)}) collective-permute-start(bf16[144,256]{1,0:T(8,128)(2,1)S(1)} %get-tuple-element.24), channel_id=1, source_target_pairs={{0,4},{1,25},{2,6},{3,27},{4,8},{5,29},{6,10},{7,31},{8,12},{9,1},... | collective-permute-start | bytes 221192 | tf_op jit(solution)/shard_map/ppermute | solution.py:435
  35.0 5.4 %collective-permute-start.3 = (bf16[144,256]{1,0:T(8,128)(2,1)S(1)}, bf16[144,256]{1,0:T(8,128)(2,1)S(1)}, u32[]{:S(2)}, u32[]{:S(2)}) collective-permute-start(bf16[144,256]{1,0:T(8,128)(2,1)S(1)} %get-tuple-element.25), channel_id=1, source_target_pairs={{0,0},{1,29},{2,2},{3,31},{4,4},{5,1},{6,6},{7,3},{8,8},{9,5},{10,... | collective-permute-start | bytes 221192 | tf_op jit(solution)/shard_map/ppermute | solution.py:435
  46.3 6.0 %collective-permute-start.4 = (bf16[16,128,256]{2,1,0:T(8,128)(2,1)S(1)}, bf16[16,128,256]{2,1,0:T(8,128)(2,1)S(1)}, u32[]{:S(2)}, u32[]{:S(2)}) collective-permute-start(bf16[16,128,256]{2,1,0:T(8,128)(2,1)S(1)} %all-to-all-done.own_ref), channel_id=1, source_target_pairs={{0,1},{1,0},{2,3},{3,2},{4,5},{5,4},{6,7},{7,6},{8,9},{9,8},{10,11... | collective-permute-start | bytes 3145736 | tf_op jit(solution)/shard_map/ppermute | solution.py:438
  50.1 2.2 %copy-start.3 = (s32[16,128]{1,0:T(8,128)S(1)}, s32[16,128]{1,0:T(8,128)}, u32[]{:S(2)}) copy-start(s32[16,128]{1,0:T(8,128)} %get-tuple-element.18.counts_ref) | copy-start | bytes 24580
  50.1 2.2 %copy-start.4 = (f32[128,128]{1,0:T(8,128)S(1)}, f32[128,128]{1,0:T(8,128)}, u32[]{:S(2)}) copy-start(f32[128,128]{1,0:T(8,128)} %constant.5.clone.sin_ref) | copy-start | bytes 196612
  50.1 2.2 %copy-start.5 = (f32[128,128]{1,0:T(8,128)S(1)}, f32[128,128]{1,0:T(8,128)}, u32[]{:S(2)}) copy-start(f32[128,128]{1,0:T(8,128)} %constant.4.clone.cos_ref) | copy-start | bytes 196612

commit v5 on v4

--- a/solution.py
+++ b/solution.py
@@ -315,21 +315,15 @@
 
 
 def attend_kernel(block, chunk, width_total, counts_ref, split_ref, queries_ref, fresh_ref, peak_ref, mixed_ref,
-                  own_ref, other_ref, gathered_ref, cos_ref, sin_ref, out_ref, blocks, live, sems):
+                  own_ref, other_ref, gathered_ref, cos_ref, sin_ref, out_ref):
     holders, slab, width = own_ref.shape
     head_dim = width // 2
     head_rows = gathered_ref.shape[1] - EXTRA
     share = 2
     rows = slab // share
     core = counts_ref[0, 1]
-    copies = [
-        pltpu.make_async_copy(ref, blocks.at[pl.ds(side * holders, holders)], sems.at[side])
-        for side, ref in enumerate((own_ref, other_ref))
-    ]
-    for copy in copies:
-        copy.start()
-    live[...] = jnp.ones(live.shape, BF16)
     spare = fresh_ref[:16, :head_dim].astype(F32)[:1]
+    spare_block = jnp.broadcast_to(spare, (rows, head_dim)).astype(BF16)
 
     position = lax.broadcasted_iota(jnp.int32, (head_rows, head_dim), 0)
     admitted = position < jnp.reshape(split_ref[...], (1, 1)) * rows
@@ -338,23 +332,20 @@
     head_values = jnp.where(admitted, values, 0.0).astype(BF16)
     head_live = jnp.where(admitted, 1.0, 0.0).astype(BF16)
 
-    def mend(side):
-        copies[side].wait()
-
-        def mend_holder(holder, _):
+    def admitted_rows(side, first, last):
+        ref = own_ref if side == 0 else other_ref
+        first_slot = (core if side == 0 else 1 - core) * share
+        keys, values, weights = [], [], []
+        for holder in range(first, last):
             for k in range(share):
-
-                @pl.when((core if side == 0 else 1 - core) * share + k >= counts_ref[holder, 0])
-                def _():
-                    here = pl.ds(k * rows, rows)
-                    place = side * holders + holder
-                    blocks[place, here, :head_dim] = jnp.broadcast_to(spare, (rows, head_dim)).astype(BF16)
-                    blocks[place, here, head_dim:] = jnp.zeros((rows, head_dim), BF16)
-                    live[place, here, :] = jnp.zeros((rows, head_dim), BF16)
-
-            return 0
-
-        lax.fori_loop(0, holders, mend_holder, 0)
+                weight = jnp.where(first_slot + k < counts_ref[holder, 0], 1.0, 0.0)
+                piece = ref[holder, k * rows : (k + 1) * rows, :]
+                keys.append(
+                    piece[:, :head_dim] * weight.astype(BF16) + spare_block * (1.0 - weight).astype(BF16)
+                )
+                values.append(piece[:, head_dim:] * weight.astype(BF16))
+                weights.append(jnp.full((rows, head_dim), weight, F32).astype(BF16))
+        return [jnp.concatenate(parts, axis=0) for parts in (keys, values, weights)]
 
     step = chunk // slab
     for b in range(queries_ref.shape[0] // block):
@@ -365,11 +356,8 @@
             for h in range(len(query))
         ]
         for start in range(0, 2 * holders, step):
-            if b == 0 and start % holders == 0:
-                mend(start // holders)
-            taken = jnp.concatenate([blocks[i] for i in range(start, start + step)], axis=0)
-            keys, values = taken[:, :head_dim], taken[:, head_dim:]
-            weights = jnp.concatenate([live[i] for i in range(start, start + step)], axis=0)
+            first = start % holders
+            keys, values, weights = admitted_rows(start // holders, first, first + step)
             if start == 0:
                 keys = jnp.concatenate([head_keys, keys], axis=0)
                 values = jnp.concatenate([head_values, values], axis=0)
@@ -387,16 +375,10 @@
     rows, width = queries.shape
     holders, slab, pair = own.shape
     cosine, sine = rotation(gathered.shape[1] - EXTRA, pair // 2)
-    anywhere = pl.BlockSpec(memory_space=pl.ANY)
     return pl.pallas_call(
-        functools.partial(attend_kernel, min(512, rows), 512, width_total),
-        in_specs=[SMEM, VMEM, VMEM, VMEM, VMEM, VMEM, anywhere, anywhere, VMEM, VMEM, VMEM],
+        functools.partial(attend_kernel, min(1024, rows), 256, width_total),
+        in_specs=[SMEM] + [VMEM] * 10,
         out_specs=VMEM,
-        scratch_shapes=[
-            pltpu.VMEM((2 * holders, slab, pair), BF16),
-            pltpu.VMEM((2 * holders, slab, pair // 2), BF16),
-            pltpu.SemaphoreType.DMA((2,)),
-        ],
         out_shape=jax.ShapeDtypeStruct((rows, width), BF16),
         compiler_params=params(24),
         cost_estimate=pl.CostEstimate(flops=2**34, bytes_accessed=2**22, transcendentals=2**23),

time: 67.5 us -> 64.3 us (0.953)
  Pallas kernels: 21.2 us -> 18 us
    pallas_call x1, Pallas kernels: 14.6 us -> 11.6 us  [attend(): pl.pallas_call(functools.partial(attend_kernel, min(1024, rows), 256, wid...]
  transfers between devices with their start and end apart: 6 -> 6, of which waited for: 1 -> 1; matrix products, arithmetic and copies ran while one was open for 0% -> 0% of each run, Pallas kernels for 3% -> 4%
where the time goes in v5:
time: 64.3 us; the launch traced here: 63.9 us
  starting transfers between devices  34.1 us (53%)
  Pallas kernels  18 us (28%)
  blocking collectives  8.54 us (13%)
  waiting for transfers between devices  2.39 us (4%)
  between operations  0.85 us (1%)
    ppermute x4, starting transfers between devices, per_device(): lax.ppermute(turn, COMP, owners_of_turn(t))  17.3 us
    all_to_all x1, starting transfers between devices, per_device(): own = lax.all_to_all(packed, POOL, split_axis=0, concat_axis=0, tiled=True)  13.7 us
    pallas_call x1, Pallas kernels, attend(): pl.pallas_call(functools.partial(attend_kernel, min(1024, rows), 256, wid...  11.6 us
    all_gather x1, blocking collectives, per_device(): gathered = lax.all_gather(join_chips(arrived), QUAD, axis=0)  5.87 us
    pallas_call x1, Pallas kernels, prepare(): pl.pallas_call(prepare_kernel, out_shape=(jax.ShapeDtypeStruct(packed, BF...  4.13 us
    ppermute x1, starting transfers between devices, per_device(): other = lax.ppermute(own, 'core', SWAP)  3.08 us
    all_gather x1, blocking collectives, per_device(): turns = join_cores(lax.all_gather(send, 'core', axis=0), keep)  2.67 us
    ppermute x4, waiting for transfers between devices, per_device(): lax.ppermute(turn, COMP, owners_of_turn(t))  2.39 us
  transfers between devices with their start and end apart: 6, of which 1 were waited for; matrix products, arithmetic and copies ran while one was open for 0% of the time, Pallas kernels for 4%

profile of v5, /device:TPU:1, one launch (start us, length us, event | category | flops | bytes accessed | tf_op | source)
XLA Modules:
  0.0 63.9 jit_solution(5022030362939243201)
XLA Ops:
  0.0 4.1 %prepare.1 = (bf16[16,128,256]{2,1,0:T(8,128)(2,1)}, bf16[4,144,256]{2,1,0:T(8,128)(2,1)}, f32[4,144,256]{2,1,0:T(8,128)}, s32[16,128]{1,0:T(8,128)}) custom-call(s32[16]{0:T(128)} %tail_ref.1, s32[16,64]{1,0:T(8,128)} %holder_ref.1, s32[16,64]{1,0:T(8,128)} %slot_ref.1, bf16[128,256]{1,0:T(8,128)(2,1)} %bitcast.14, bf16[256]{0:T(256)(128)(2,1)} %gain_ref.1, ...), custom_call_target="tpu_custom_call" | custom-call | tf_op jit(solution)/shard_map/prepare/pallas_call | solution.py:159
  4.1 0.0 copy-start.6
  4.1 0.0 copy-start
  4.2 0.0 copy-start.1
  4.2 0.0 copy-start.2
  4.2 13.7 %all-to-all-start = ((bf16[16,128,256]{2,1,0:T(8,128)(2,1)}), bf16[16,128,256]{2,1,0:T(8,128)(2,1)S(1)}, u32[]{:S(2)}, u32[]{:S(2)}) async-start(bf16[16,128,256]{2,1,0:T(8,128)(2,1)} %get-tuple-element.19), calls=%async_computation | async-start | bytes 2097152 | tf_op jit(solution)/shard_map/all_to_all | solution.py:415
  17.9 0.0 copy-done.6
  17.9 2.7 %all-gather = bf16[8,144,256]{2,1,0:T(8,128)(2,1)S(1)} all-gather(bf16[4,144,256]{2,1,0:T(8,128)(2,1)S(1)} %copy-done.6), channel_id=2, replica_groups=mesh['xh'=2,'z'=8,'y'=8,'xl'=2,'core'=2] {'core'}, dimensions={0}, use_global_device_ids=true | all-gather | bytes 884736 | tf_op jit(solution)/shard_map/all_gather | solution.py:416
  20.6 0.0 copy-done
  20.6 0.1 join_cores.1
  20.6 7.5 %collective-permute-start = (bf16[144,256]{1,0:T(8,128)(2,1)S(1)}, bf16[144,256]{1,0:T(8,128)(2,1)S(1)}, u32[]{:S(2)}, u32[]{:S(2)}) collective-permute-start(bf16[144,256]{1,0:T(8,128)(2,1)S(1)} %get-tuple-element.22), channel_id=1, source_target_pairs={{0,12},{1,17},{2,14},{3,19},{4,16},{5,21},{6,18},{7,23},{8,20},{9,... | collective-permute-start | bytes 221192 | tf_op jit(solution)/shard_map/ppermute | solution.py:417
  28.1 1.9 %collective-permute-start.1 = (bf16[144,256]{1,0:T(8,128)(2,1)S(1)}, bf16[144,256]{1,0:T(8,128)(2,1)S(1)}, u32[]{:S(2)}, u32[]{:S(2)}) collective-permute-start(bf16[144,256]{1,0:T(8,128)(2,1)S(1)} %get-tuple-element.23), channel_id=1, source_target_pairs={{0,8},{1,21},{2,10},{3,23},{4,12},{5,25},{6,14},{7,27},{8,16},{9,2... | collective-permute-start | bytes 221192 | tf_op jit(solution)/shard_map/ppermute | solution.py:417
  30.0 4.9 %collective-permute-start.2 = (bf16[144,256]{1,0:T(8,128)(2,1)S(1)}, bf16[144,256]{1,0:T(8,128)(2,1)S(1)}, u32[]{:S(2)}, u32[]{:S(2)}) collective-permute-start(bf16[144,256]{1,0:T(8,128)(2,1)S(1)} %get-tuple-element.24), channel_id=1, source_target_pairs={{0,4},{1,25},{2,6},{3,27},{4,8},{5,29},{6,10},{7,31},{8,12},{9,1},... | collective-permute-start | bytes 221192 | tf_op jit(solution)/shard_map/ppermute | solution.py:417
  35.0 3.0 %collective-permute-start.3 = (bf16[144,256]{1,0:T(8,128)(2,1)S(1)}, bf16[144,256]{1,0:T(8,128)(2,1)S(1)}, u32[]{:S(2)}, u32[]{:S(2)}) collective-permute-start(bf16[144,256]{1,0:T(8,128)(2,1)S(1)} %get-tuple-element.25), channel_id=1, source_target_pairs={{0,0},{1,29},{2,2},{3,31},{4,4},{5,1},{6,6},{7,3},{8,8},{9,5},{10,... | collective-permute-start | bytes 221192 | tf_op jit(solution)/shard_map/ppermute | solution.py:417
  37.9 0.0 collective-permute-done.refs_0_
  38.0 0.0 collective-permute-done.1.refs_1_
  38.0 0.0 collective-permute-done.2.refs_2_
  38.0 2.4 %collective-permute-done.3.refs_3_ = bf16[144,256]{1,0:T(8,128)(2,1)S(1)} collective-permute-done((bf16[144,256]{1,0:T(8,128)(2,1)S(1)}, bf16[144,256]{1,0:T(8,128)(2,1)S(1)}, u32[]{:S(2)}, u32[]{:S(2)}) %collective-permute-start.3) | collective-permute-done | bytes 73760 | tf_op jit(solution)/shard_map/ppermute | solution.py:417
  40.4 5.9 %all-gather.1 = bf16[576,256]{1,0:T(8,128)(2,1)S(1)} all-gather(bf16[144,256]{1,0:T(8,128)(2,1)S(1)} %join_chips.1), channel_id=3, replica_groups=mesh['xh'=2,'z'=8,'y'=8,'xl'=2,'core'=2] {'xl','core'}, dimensions={0}, use_global_device_ids=true | all-gather | bytes 368640 | tf_op jit(solution)/shard_map/all_gather | solution.py:418
  46.3 0.0 all-to-all-done.own_ref
  46.3 3.1 %collective-permute-start.4 = (bf16[16,128,256]{2,1,0:T(8,128)(2,1)S(1)}, bf16[16,128,256]{2,1,0:T(8,128)(2,1)S(1)}, u32[]{:S(2)}, u32[]{:S(2)}) collective-permute-start(bf16[16,128,256]{2,1,0:T(8,128)(2,1)S(1)} %all-to-all-done.own_ref), channel_id=1, source_target_pairs={{0,1},{1,0},{2,3},{3,2},{4,5},{5,4},{6,7},{7,6},{8,9},{9,8},{10,11... | collective-permute-start | bytes 3145736 | tf_op jit(solution)/shard_map/ppermute | solution.py:420
  50.0 0.0 copy-done.1
  50.0 0.0 copy-done.2
  50.0 0.0 copy-start.3
  50.0 0.0 copy-start.4
  50.0 0.0 copy-start.5
  50.1 2.2 %attend_fresh.1 = (f32[2,1024,128]{2,1,0:T(8,128)S(1)}, f32[2,1024,256]{2,1,0:T(8,128)S(1)}) custom-call(bf16[1024,256]{1,0:T(8,128)(2,1)S(1)} %bitcast.9, bf16[1024,256]{1,0:T(8,128)(2,1)S(1)} %bitcast.11), custom_call_target="tpu_custom_call" | custom-call | flops 2147483648 | bytes 2097152 | tf_op jit(solution)/shard_map/attend_fresh/pallas_call | solution.py:303
  52.3 0.0 collective-permute-done.4.other_ref
  52.3 0.0 copy-done.3
  52.3 0.0 copy-done.4
  52.3 0.0 copy-done.5
  52.3 11.6 %attend.1 = bf16[1024,256]{1,0:T(8,128)(2,1)} custom-call(s32[16,128]{1,0:T(8,128)S(1)} %copy-done.3, s32[1]{0:T(128)S(6)} %copy.13.split_ref, bf16[1024,256]{1,0:T(8,128)(2,1)S(1)} %bitcast.10, bf16[1024,256]{1,0:T(8,128)(2,1)S(1)} %bitcast.12, f32[2,1024,128]{2,1,0:T(8,128)S(1)} %get-tuple-element.27.peak_ref, ...), custom_call_target="tpu_custom_call" | custom-call | flops 17179869184 | bytes 4194304 | tf_op jit(solution)/shard_map/attend/pallas_call | solution.py:378
  (1 shorter events, 0.0 us)
Async XLA Ops:
  4.1 13.8 %copy-start.6 = (bf16[4,144,256]{2,1,0:T(8,128)(2,1)S(1)}, bf16[4,144,256]{2,1,0:T(8,128)(2,1)}, u32[]{:S(2)}) copy-start(bf16[4,144,256]{2,1,0:T(8,128)(2,1)} %get-tuple-element.20) | copy-start | bytes 884740
  4.1 16.4 %copy-start = (f32[4,144,256]{2,1,0:T(8,128)S(1)}, f32[4,144,256]{2,1,0:T(8,128)}, u32[]{:S(2)}) copy-start(f32[4,144,256]{2,1,0:T(8,128)} %get-tuple-element.21.mine_ref) | copy-start | bytes 1769476
  4.2 45.8 %copy-start.1 = (bf16[1,1024,256]{2,1,0:T(8,128)(2,1)S(1)}, bf16[1,1024,256]{2,1,0:T(8,128)(2,1)}, u32[]{:S(2)}) copy-start(bf16[1,1024,256]{2,1,0:T(8,128)(2,1)} %param.12) | copy-start | bytes 1572868
  4.2 45.8 %copy-start.2 = (bf16[1,1024,1,256]{3,1,2,0:T(8,128)(2,1)S(1)}, bf16[1,1024,1,256]{3,1,2,0:T(8,128)(2,1)}, u32[]{:S(2)}) copy-start(bf16[1,1024,1,256]{3,1,2,0:T(8,128)(2,1)} %param.13) | copy-start | bytes 1572868
  4.2 42.1 %all-to-all-start = ((bf16[16,128,256]{2,1,0:T(8,128)(2,1)}), bf16[16,128,256]{2,1,0:T(8,128)(2,1)S(1)}, u32[]{:S(2)}, u32[]{:S(2)}) async-start(bf16[16,128,256]{2,1,0:T(8,128)(2,1)} %get-tuple-element.19), calls=%async_computation | async-start | bytes 2097152 | tf_op jit(solution)/shard_map/all_to_all | solution.py:415
  20.6 17.3 %collective-permute-start = (bf16[144,256]{1,0:T(8,128)(2,1)S(1)}, bf16[144,256]{1,0:T(8,128)(2,1)S(1)}, u32[]{:S(2)}, u32[]{:S(2)}) collective-permute-start(bf16[144,256]{1,0:T(8,128)(2,1)S(1)} %get-tuple-element.22), channel_id=1, source_target_pairs={{0,12},{1,17},{2,14},{3,19},{4,16},{5,21},{6,18},{7,23},{8,20},{9,... | collective-permute-start | bytes 221192 | tf_op jit(solution)/shard_map/ppermute | solution.py:417
  28.1 9.8 %collective-permute-start.1 = (bf16[144,256]{1,0:T(8,128)(2,1)S(1)}, bf16[144,256]{1,0:T(8,128)(2,1)S(1)}, u32[]{:S(2)}, u32[]{:S(2)}) collective-permute-start(bf16[144,256]{1,0:T(8,128)(2,1)S(1)} %get-tuple-element.23), channel_id=1, source_target_pairs={{0,8},{1,21},{2,10},{3,23},{4,12},{5,25},{6,14},{7,27},{8,16},{9,2... | collective-permute-start | bytes 221192 | tf_op jit(solution)/shard_map/ppermute | solution.py:417
  30.0 7.9 %collective-permute-start.2 = (bf16[144,256]{1,0:T(8,128)(2,1)S(1)}, bf16[144,256]{1,0:T(8,128)(2,1)S(1)}, u32[]{:S(2)}, u32[]{:S(2)}) collective-permute-start(bf16[144,256]{1,0:T(8,128)(2,1)S(1)} %get-tuple-element.24), channel_id=1, source_target_pairs={{0,4},{1,25},{2,6},{3,27},{4,8},{5,29},{6,10},{7,31},{8,12},{9,1},... | collective-permute-start | bytes 221192 | tf_op jit(solution)/shard_map/ppermute | solution.py:417
  35.0 5.4 %collective-permute-start.3 = (bf16[144,256]{1,0:T(8,128)(2,1)S(1)}, bf16[144,256]{1,0:T(8,128)(2,1)S(1)}, u32[]{:S(2)}, u32[]{:S(2)}) collective-permute-start(bf16[144,256]{1,0:T(8,128)(2,1)S(1)} %get-tuple-element.25), channel_id=1, source_target_pairs={{0,0},{1,29},{2,2},{3,31},{4,4},{5,1},{6,6},{7,3},{8,8},{9,5},{10,... | collective-permute-start | bytes 221192 | tf_op jit(solution)/shard_map/ppermute | solution.py:417
  46.3 6.0 %collective-permute-start.4 = (bf16[16,128,256]{2,1,0:T(8,128)(2,1)S(1)}, bf16[16,128,256]{2,1,0:T(8,128)(2,1)S(1)}, u32[]{:S(2)}, u32[]{:S(2)}) collective-permute-start(bf16[16,128,256]{2,1,0:T(8,128)(2,1)S(1)} %all-to-all-done.own_ref), channel_id=1, source_target_pairs={{0,1},{1,0},{2,3},{3,2},{4,5},{5,4},{6,7},{7,6},{8,9},{9,8},{10,11... | collective-permute-start | bytes 3145736 | tf_op jit(solution)/shard_map/ppermute | solution.py:420
  50.0 2.2 %copy-start.3 = (s32[16,128]{1,0:T(8,128)S(1)}, s32[16,128]{1,0:T(8,128)}, u32[]{:S(2)}) copy-start(s32[16,128]{1,0:T(8,128)} %get-tuple-element.18.counts_ref) | copy-start | bytes 24580
  50.0 2.2 %copy-start.4 = (f32[128,128]{1,0:T(8,128)S(1)}, f32[128,128]{1,0:T(8,128)}, u32[]{:S(2)}) copy-start(f32[128,128]{1,0:T(8,128)} %constant.5.clone.sin_ref) | copy-start | bytes 196612
  50.0 2.2 %copy-start.5 = (f32[128,128]{1,0:T(8,128)S(1)}, f32[128,128]{1,0:T(8,128)}, u32[]{:S(2)}) copy-start(f32[128,128]{1,0:T(8,128)} %constant.4.clone.cos_ref) | copy-start | bytes 196612

commit v6 on v5

--- a/solution.py
+++ b/solution.py
@@ -301,7 +301,7 @@
     rows, width = queries.shape
     heads = 2 * width // fresh.shape[1]
     return pl.pallas_call(
-        functools.partial(fresh_kernel, min(512, rows)),
+        functools.partial(fresh_kernel, min(256, rows)),
         in_specs=[VMEM, VMEM],
         out_specs=(VMEM, VMEM),
         out_shape=(

time: 64.3 us -> 64.1 us (level)
  transfers between devices with their start and end apart: 6 -> 6, of which waited for: 1 -> 1; matrix products, arithmetic and copies ran while one was open for 0% -> 0% of each run, Pallas kernels for 4% -> 3%
where the time goes in v6:
time: 64.1 us; the launch traced here: 63.6 us
  starting transfers between devices  33.9 us (53%)
  Pallas kernels  17.9 us (28%)
  blocking collectives  8.58 us (13%)
  waiting for transfers between devices  2.39 us (4%)
  between operations  0.85 us (1%)
    ppermute x4, starting transfers between devices, per_device(): lax.ppermute(turn, COMP, owners_of_turn(t))  17.3 us
    all_to_all x1, starting transfers between devices, per_device(): own = lax.all_to_all(packed, POOL, split_axis=0, concat_axis=0, tiled=True)  13.6 us
    pallas_call x1, Pallas kernels, attend(): pl.pallas_call(functools.partial(attend_kernel, min(1024, rows), 256, wid...  11.6 us
    all_gather x1, blocking collectives, per_device(): gathered = lax.all_gather(join_chips(arrived), QUAD, axis=0)  5.84 us
    pallas_call x1, Pallas kernels, prepare(): pl.pallas_call(prepare_kernel, out_shape=(jax.ShapeDtypeStruct(packed, BF...  4.18 us
    ppermute x1, starting transfers between devices, per_device(): other = lax.ppermute(own, 'core', SWAP)  3.02 us
    all_gather x1, blocking collectives, per_device(): turns = join_cores(lax.all_gather(send, 'core', axis=0), keep)  2.75 us
    ppermute x4, waiting for transfers between devices, per_device(): lax.ppermute(turn, COMP, owners_of_turn(t))  2.39 us
  transfers between devices with their start and end apart: 6, of which 1 were waited for; matrix products, arithmetic and copies ran while one was open for 0% of the time, Pallas kernels for 3%

profile of v6, /device:TPU:1, one launch (start us, length us, event | category | flops | bytes accessed | tf_op | source)
XLA Modules:
  0.0 63.6 jit_solution(10535857290735857807)
XLA Ops:
  0.0 4.2 %prepare.1 = (bf16[16,128,256]{2,1,0:T(8,128)(2,1)}, bf16[4,144,256]{2,1,0:T(8,128)(2,1)}, f32[4,144,256]{2,1,0:T(8,128)}, s32[16,128]{1,0:T(8,128)}) custom-call(s32[16]{0:T(128)} %tail_ref.1, s32[16,64]{1,0:T(8,128)} %holder_ref.1, s32[16,64]{1,0:T(8,128)} %slot_ref.1, bf16[128,256]{1,0:T(8,128)(2,1)} %bitcast.14, bf16[256]{0:T(256)(128)(2,1)} %gain_ref.1, ...), custom_call_target="tpu_custom_call" | custom-call | tf_op jit(solution)/shard_map/prepare/pallas_call | solution.py:159
  4.2 0.0 copy-start.6
  4.2 0.0 copy-start
  4.2 0.0 copy-start.1
  4.2 0.0 copy-start.2
  4.2 13.6 %all-to-all-start = ((bf16[16,128,256]{2,1,0:T(8,128)(2,1)}), bf16[16,128,256]{2,1,0:T(8,128)(2,1)S(1)}, u32[]{:S(2)}, u32[]{:S(2)}) async-start(bf16[16,128,256]{2,1,0:T(8,128)(2,1)} %get-tuple-element.19), calls=%async_computation | async-start | bytes 2097152 | tf_op jit(solution)/shard_map/all_to_all | solution.py:415
  17.8 0.0 copy-done.6
  17.8 2.7 %all-gather = bf16[8,144,256]{2,1,0:T(8,128)(2,1)S(1)} all-gather(bf16[4,144,256]{2,1,0:T(8,128)(2,1)S(1)} %copy-done.6), channel_id=2, replica_groups=mesh['xh'=2,'z'=8,'y'=8,'xl'=2,'core'=2] {'core'}, dimensions={0}, use_global_device_ids=true | all-gather | bytes 884736 | tf_op jit(solution)/shard_map/all_gather | solution.py:416
  20.6 0.0 copy-done
  20.6 0.1 join_cores.1
  20.6 7.5 %collective-permute-start = (bf16[144,256]{1,0:T(8,128)(2,1)S(1)}, bf16[144,256]{1,0:T(8,128)(2,1)S(1)}, u32[]{:S(2)}, u32[]{:S(2)}) collective-permute-start(bf16[144,256]{1,0:T(8,128)(2,1)S(1)} %get-tuple-element.22), channel_id=1, source_target_pairs={{0,12},{1,17},{2,14},{3,19},{4,16},{5,21},{6,18},{7,23},{8,20},{9,... | collective-permute-start | bytes 221192 | tf_op jit(solution)/shard_map/ppermute | solution.py:417
  28.1 1.9 %collective-permute-start.1 = (bf16[144,256]{1,0:T(8,128)(2,1)S(1)}, bf16[144,256]{1,0:T(8,128)(2,1)S(1)}, u32[]{:S(2)}, u32[]{:S(2)}) collective-permute-start(bf16[144,256]{1,0:T(8,128)(2,1)S(1)} %get-tuple-element.23), channel_id=1, source_target_pairs={{0,8},{1,21},{2,10},{3,23},{4,12},{5,25},{6,14},{7,27},{8,16},{9,2... | collective-permute-start | bytes 221192 | tf_op jit(solution)/shard_map/ppermute | solution.py:417
  30.0 4.9 %collective-permute-start.2 = (bf16[144,256]{1,0:T(8,128)(2,1)S(1)}, bf16[144,256]{1,0:T(8,128)(2,1)S(1)}, u32[]{:S(2)}, u32[]{:S(2)}) collective-permute-start(bf16[144,256]{1,0:T(8,128)(2,1)S(1)} %get-tuple-element.24), channel_id=1, source_target_pairs={{0,4},{1,25},{2,6},{3,27},{4,8},{5,29},{6,10},{7,31},{8,12},{9,1},... | collective-permute-start | bytes 221192 | tf_op jit(solution)/shard_map/ppermute | solution.py:417
  35.0 3.0 %collective-permute-start.3 = (bf16[144,256]{1,0:T(8,128)(2,1)S(1)}, bf16[144,256]{1,0:T(8,128)(2,1)S(1)}, u32[]{:S(2)}, u32[]{:S(2)}) collective-permute-start(bf16[144,256]{1,0:T(8,128)(2,1)S(1)} %get-tuple-element.25), channel_id=1, source_target_pairs={{0,0},{1,29},{2,2},{3,31},{4,4},{5,1},{6,6},{7,3},{8,8},{9,5},{10,... | collective-permute-start | bytes 221192 | tf_op jit(solution)/shard_map/ppermute | solution.py:417
  37.9 0.0 collective-permute-done.refs_0_
  38.0 0.0 collective-permute-done.1.refs_1_
  38.0 0.0 collective-permute-done.2.refs_2_
  38.0 2.4 %collective-permute-done.3.refs_3_ = bf16[144,256]{1,0:T(8,128)(2,1)S(1)} collective-permute-done((bf16[144,256]{1,0:T(8,128)(2,1)S(1)}, bf16[144,256]{1,0:T(8,128)(2,1)S(1)}, u32[]{:S(2)}, u32[]{:S(2)}) %collective-permute-start.3) | collective-permute-done | bytes 73760 | tf_op jit(solution)/shard_map/ppermute | solution.py:417
  40.4 5.8 %all-gather.1 = bf16[576,256]{1,0:T(8,128)(2,1)S(1)} all-gather(bf16[144,256]{1,0:T(8,128)(2,1)S(1)} %join_chips.1), channel_id=3, replica_groups=mesh['xh'=2,'z'=8,'y'=8,'xl'=2,'core'=2] {'xl','core'}, dimensions={0}, use_global_device_ids=true | all-gather | bytes 368640 | tf_op jit(solution)/shard_map/all_gather | solution.py:418
  46.2 0.0 all-to-all-done.own_ref
  46.2 3.0 %collective-permute-start.4 = (bf16[16,128,256]{2,1,0:T(8,128)(2,1)S(1)}, bf16[16,128,256]{2,1,0:T(8,128)(2,1)S(1)}, u32[]{:S(2)}, u32[]{:S(2)}) collective-permute-start(bf16[16,128,256]{2,1,0:T(8,128)(2,1)S(1)} %all-to-all-done.own_ref), channel_id=1, source_target_pairs={{0,1},{1,0},{2,3},{3,2},{4,5},{5,4},{6,7},{7,6},{8,9},{9,8},{10,11... | collective-permute-start | bytes 3145736 | tf_op jit(solution)/shard_map/ppermute | solution.py:420
  49.9 0.0 copy-done.1
  49.9 0.0 copy-done.2
  49.9 0.0 copy-start.3
  49.9 0.0 copy-start.4
  50.0 0.0 copy-start.5
  50.0 2.0 %attend_fresh.1 = (f32[2,1024,128]{2,1,0:T(8,128)S(1)}, f32[2,1024,256]{2,1,0:T(8,128)S(1)}) custom-call(bf16[1024,256]{1,0:T(8,128)(2,1)S(1)} %bitcast.9, bf16[1024,256]{1,0:T(8,128)(2,1)S(1)} %bitcast.11), custom_call_target="tpu_custom_call" | custom-call | flops 2147483648 | bytes 2097152 | tf_op jit(solution)/shard_map/attend_fresh/pallas_call | solution.py:303
  52.0 0.0 collective-permute-done.4.other_ref
  52.0 0.0 copy-done.3
  52.0 0.0 copy-done.4
  52.0 0.0 copy-done.5
  52.0 11.6 %attend.1 = bf16[1024,256]{1,0:T(8,128)(2,1)} custom-call(s32[16,128]{1,0:T(8,128)S(1)} %copy-done.3, s32[1]{0:T(128)S(6)} %copy.13.split_ref, bf16[1024,256]{1,0:T(8,128)(2,1)S(1)} %bitcast.10, bf16[1024,256]{1,0:T(8,128)(2,1)S(1)} %bitcast.12, f32[2,1024,128]{2,1,0:T(8,128)S(1)} %get-tuple-element.27.peak_ref, ...), custom_call_target="tpu_custom_call" | custom-call | flops 17179869184 | bytes 4194304 | tf_op jit(solution)/shard_map/attend/pallas_call | solution.py:378
  (1 shorter events, 0.0 us)
Async XLA Ops:
  4.2 13.6 %copy-start.6 = (bf16[4,144,256]{2,1,0:T(8,128)(2,1)S(1)}, bf16[4,144,256]{2,1,0:T(8,128)(2,1)}, u32[]{:S(2)}) copy-start(bf16[4,144,256]{2,1,0:T(8,128)(2,1)} %get-tuple-element.20) | copy-start | bytes 884740
  4.2 16.4 %copy-start = (f32[4,144,256]{2,1,0:T(8,128)S(1)}, f32[4,144,256]{2,1,0:T(8,128)}, u32[]{:S(2)}) copy-start(f32[4,144,256]{2,1,0:T(8,128)} %get-tuple-element.21.mine_ref) | copy-start | bytes 1769476
  4.2 45.7 %copy-start.1 = (bf16[1,1024,256]{2,1,0:T(8,128)(2,1)S(1)}, bf16[1,1024,256]{2,1,0:T(8,128)(2,1)}, u32[]{:S(2)}) copy-start(bf16[1,1024,256]{2,1,0:T(8,128)(2,1)} %param.12) | copy-start | bytes 1572868
  4.2 45.7 %copy-start.2 = (bf16[1,1024,1,256]{3,1,2,0:T(8,128)(2,1)S(1)}, bf16[1,1024,1,256]{3,1,2,0:T(8,128)(2,1)}, u32[]{:S(2)}) copy-start(bf16[1,1024,1,256]{3,1,2,0:T(8,128)(2,1)} %param.13) | copy-start | bytes 1572868
  4.2 42.0 %all-to-all-start = ((bf16[16,128,256]{2,1,0:T(8,128)(2,1)}), bf16[16,128,256]{2,1,0:T(8,128)(2,1)S(1)}, u32[]{:S(2)}, u32[]{:S(2)}) async-start(bf16[16,128,256]{2,1,0:T(8,128)(2,1)} %get-tuple-element.19), calls=%async_computation | async-start | bytes 2097152 | tf_op jit(solution)/shard_map/all_to_all | solution.py:415
  20.6 17.3 %collective-permute-start = (bf16[144,256]{1,0:T(8,128)(2,1)S(1)}, bf16[144,256]{1,0:T(8,128)(2,1)S(1)}, u32[]{:S(2)}, u32[]{:S(2)}) collective-permute-start(bf16[144,256]{1,0:T(8,128)(2,1)S(1)} %get-tuple-element.22), channel_id=1, source_target_pairs={{0,12},{1,17},{2,14},{3,19},{4,16},{5,21},{6,18},{7,23},{8,20},{9,... | collective-permute-start | bytes 221192 | tf_op jit(solution)/shard_map/ppermute | solution.py:417
  28.1 9.8 %collective-permute-start.1 = (bf16[144,256]{1,0:T(8,128)(2,1)S(1)}, bf16[144,256]{1,0:T(8,128)(2,1)S(1)}, u32[]{:S(2)}, u32[]{:S(2)}) collective-permute-start(bf16[144,256]{1,0:T(8,128)(2,1)S(1)} %get-tuple-element.23), channel_id=1, source_target_pairs={{0,8},{1,21},{2,10},{3,23},{4,12},{5,25},{6,14},{7,27},{8,16},{9,2... | collective-permute-start | bytes 221192 | tf_op jit(solution)/shard_map/ppermute | solution.py:417
  30.0 7.9 %collective-permute-start.2 = (bf16[144,256]{1,0:T(8,128)(2,1)S(1)}, bf16[144,256]{1,0:T(8,128)(2,1)S(1)}, u32[]{:S(2)}, u32[]{:S(2)}) collective-permute-start(bf16[144,256]{1,0:T(8,128)(2,1)S(1)} %get-tuple-element.24), channel_id=1, source_target_pairs={{0,4},{1,25},{2,6},{3,27},{4,8},{5,29},{6,10},{7,31},{8,12},{9,1},... | collective-permute-start | bytes 221192 | tf_op jit(solution)/shard_map/ppermute | solution.py:417
  35.0 5.4 %collective-permute-start.3 = (bf16[144,256]{1,0:T(8,128)(2,1)S(1)}, bf16[144,256]{1,0:T(8,128)(2,1)S(1)}, u32[]{:S(2)}, u32[]{:S(2)}) collective-permute-start(bf16[144,256]{1,0:T(8,128)(2,1)S(1)} %get-tuple-element.25), channel_id=1, source_target_pairs={{0,0},{1,29},{2,2},{3,31},{4,4},{5,1},{6,6},{7,3},{8,8},{9,5},{10,... | collective-permute-start | bytes 221192 | tf_op jit(solution)/shard_map/ppermute | solution.py:417
  46.2 5.8 %collective-permute-start.4 = (bf16[16,128,256]{2,1,0:T(8,128)(2,1)S(1)}, bf16[16,128,256]{2,1,0:T(8,128)(2,1)S(1)}, u32[]{:S(2)}, u32[]{:S(2)}) collective-permute-start(bf16[16,128,256]{2,1,0:T(8,128)(2,1)S(1)} %all-to-all-done.own_ref), channel_id=1, source_target_pairs={{0,1},{1,0},{2,3},{3,2},{4,5},{5,4},{6,7},{7,6},{8,9},{9,8},{10,11... | collective-permute-start | bytes 3145736 | tf_op jit(solution)/shard_map/ppermute | solution.py:420
  49.9 2.1 %copy-start.3 = (s32[16,128]{1,0:T(8,128)S(1)}, s32[16,128]{1,0:T(8,128)}, u32[]{:S(2)}) copy-start(s32[16,128]{1,0:T(8,128)} %get-tuple-element.18.counts_ref) | copy-start | bytes 24580
  49.9 2.1 %copy-start.4 = (f32[128,128]{1,0:T(8,128)S(1)}, f32[128,128]{1,0:T(8,128)}, u32[]{:S(2)}) copy-start(f32[128,128]{1,0:T(8,128)} %constant.5.clone.sin_ref) | copy-start | bytes 196612
  50.0 2.1 %copy-start.5 = (f32[128,128]{1,0:T(8,128)S(1)}, f32[128,128]{1,0:T(8,128)}, u32[]{:S(2)}) copy-start(f32[128,128]{1,0:T(8,128)} %constant.4.clone.cos_ref) | copy-start | bytes 196612
